TPU v7x, 32 devices: a whole 2x2x4 slice. The times are simulated.
32 devices in a mesh: sys: 4 (over y, x), edge: 8 (over z, core).
Axes of the slice: x: 2, y: 2, z: 4, core: 2. Of those that a mesh axis runs over, the one named last changes fastest.
Arguments:
- positions: float32 [3, 4096], P(None, ('sys', 'edge')), may hold values from 0 to 2.5
- velocities: float32 [3, 4096], P(None, ('sys', 'edge')), may hold values from -3 to 3
- species: int32 [4096], P(('sys', 'edge')), may hold values from 0 to 3
- senders: int32 [3, 32768], P(None, ('sys', 'edge')), may hold values from 0 to 127, as said below
- receivers: int32 [3, 32768], P(None, ('sys', 'edge')), may hold values from 0 to 127, as said below
- edge_mask: int32 [3, 32768], P(None, ('sys', 'edge')), may hold values 0 or 1
- embedding: float32 [4, 64], replicated, may hold values from -4 to 4
- radial_in: float32 [2, 8, 64], replicated, may hold values from -4 to 4
- radial_out: float32 [2, 64, 192], replicated, may hold values from -0.75 to 0.75
- mix_first: float32 [64, 192], replicated, may hold values from -0.75 to 0.75
- mix_square: float32 [3, 64, 64], replicated, may hold values from -0.75 to 0.75
- readout: float32 [64], replicated, may hold values from -0.75 to 0.75
- embedding_rows: float32 [4], replicated, may hold values from 1e-05 to 0.01
- embedding_cols: float32 [64], replicated, may hold values from 1e-05 to 0.01
- radial_in_rows: float32 [2, 8], replicated, may hold values from 1e-05 to 0.01
- radial_in_cols: float32 [2, 64], replicated, may hold values from 1e-05 to 0.01
- radial_out_rows: float32 [2, 64], replicated, may hold values from 1e-05 to 0.01
- radial_out_cols: float32 [2, 192], replicated, may hold values from 1e-05 to 0.01
- mix_first_rows: float32 [64], replicated, may hold values from 1e-05 to 0.01
- mix_first_cols: float32 [192], replicated, may hold values from 1e-05 to 0.01
- mix_square_rows: float32 [3, 64], replicated, may hold values from 1e-05 to 0.01
- mix_square_cols: float32 [3, 64], replicated, may hold values from 1e-05 to 0.01
- readout_second: float32 [64], replicated, may hold values from 1e-05 to 0.01
Outputs:
- loss_total: float32 [], replicated
- embedding_grad: float32 [4, 64], replicated
- embedding_rows_new: float32 [4], replicated
- embedding_cols_new: float32 [64], replicated
- embedding_new: float32 [4, 64], replicated
- embedding_half: bfloat16 [4, 64], replicated
- radial_in_grad: float32 [2, 8, 64], replicated
- radial_in_rows_new: float32 [2, 8], replicated
- radial_in_cols_new: float32 [2, 64], replicated
- radial_in_new: float32 [2, 8, 64], replicated
- radial_in_half: bfloat16 [2, 8, 64], replicated
- radial_out_grad: float32 [2, 64, 192], replicated
- radial_out_rows_new: float32 [2, 64], replicated
- radial_out_cols_new: float32 [2, 192], replicated
- radial_out_new: float32 [2, 64, 192], replicated
- radial_out_half: bfloat16 [2, 64, 192], replicated
- mix_first_grad: float32 [64, 192], replicated
- mix_first_rows_new: float32 [64], replicated
- mix_first_cols_new: float32 [192], replicated
- mix_first_new: float32 [64, 192], replicated
- mix_first_half: bfloat16 [64, 192], replicated
- mix_square_grad: float32 [3, 64, 64], replicated
- mix_square_rows_new: float32 [3, 64], replicated
- mix_square_cols_new: float32 [3, 64], replicated
- mix_square_new: float32 [3, 64, 64], replicated
- mix_square_half: bfloat16 [3, 64, 64], replicated
- readout_grad: float32 [64], replicated
- readout_second_new: float32 [64], replicated
- readout_new: float32 [64], replicated
- readout_half: bfloat16 [64], replicated
Inputs may be any that keep to these rules, and one draw needn't show every extreme that they name: `senders`: A sender is an atom of the device that holds the edge slot. receivers[k, s] // 64 == senders[k, s] // 64: an edge joins two atoms of one system.
All inputs are finite; a program needn't handle non-finite values. No bound on the sum of `edge_mask` on one device may be relied on, other than what follows from the above.
Results may differ from a plain program's by a relative error of at most 0.001.
Values sent between devices are 32-bit elements; how exact they have to be, the bound alone decides.
A program may use at most 256 MiB of HBM per device.

v0:
```python
from functools import reduce
import math

import jax
import jax.numpy as jnp
from jax import lax
from jax.experimental import pallas as pl
from jax.experimental.pallas import tpu as pltpu
from jax.sharding import PartitionSpec as P

NB = 8
SYS_LOC = 2
STEPS = 2
STEP_NUM = 10
EVALS = 3


PRECISE = lax.Precision.HIGHEST
SOFTEN = 0.25
CUTOFF = 5.0
INV_NEIGH = 0.2
STEP_DT = 0.5
RELATIVE = 0.3
EPS_SQUARE = 1e-30
ROOT3 = math.sqrt(3.0)
ROOT5 = math.sqrt(5.0)


def geometry(sender_pos, receiver_pos):
    offset_vec = sender_pos - receiver_pos
    radius = jnp.sqrt(jnp.sum(offset_vec * offset_vec, axis=0) + SOFTEN)
    direction = offset_vec / radius
    unit_x, unit_y, unit_z = (direction[0], direction[1], direction[2])
    first_harm = ROOT3 * direction
    second_harm = ROOT5 * jnp.stack(
        [
            ROOT3 * unit_x * unit_y,
            ROOT3 * unit_y * unit_z,
            0.5 * (3.0 * unit_z * unit_z - 1.0),
            ROOT3 * unit_x * unit_z,
            0.5 * ROOT3 * (unit_x * unit_x - unit_y * unit_y),
        ]
    )
    scaled = radius / CUTOFF
    envelope = 1.0 - 28.0 * scaled**6 + 48.0 * scaled**7 - 21.0 * scaled**8
    orders = jnp.arange(1, NB + 1).astype(jnp.float32)[:, None]
    bessel = (
        math.sqrt(2.0 / CUTOFF)
        * jnp.sin(orders * math.pi * scaled[None, :])
        / radius[None, :]
        * envelope[None, :]
    )
    return (first_harm, second_harm, bessel)


def radial(bessel, weight_in, weight_out):
    hidden = jax.nn.silu(jnp.einsum("nr,ne->re", weight_in, bessel, precision=PRECISE))
    return jnp.einsum("rk,re->ke", weight_out, hidden, precision=PRECISE)


def first_messages(
    first_harm, second_harm, bessel, sender_feat, edge_weight, weight_in, weight_out
):
    channels = sender_feat.shape[0]
    edge_weights = radial(bessel, weight_in, weight_out)
    scalar_part = (edge_weights[:channels] * sender_feat)[None]
    vector_part = (edge_weights[channels : 2 * channels] * sender_feat)[None] * first_harm[
        :, None, :
    ]
    tensor_part = (edge_weights[2 * channels :] * sender_feat)[None] * second_harm[:, None, :]
    return jnp.concatenate([scalar_part, vector_part, tensor_part], axis=0) * edge_weight


def node_first(summed, scalar_prev, mix_first, mix_square):
    gathered = summed * INV_NEIGH
    channels = scalar_prev.shape[0]
    mixed = jnp.einsum("cd,ca->da", mix_first, gathered[0], precision=PRECISE)
    vectors = jnp.einsum("mca,cd->mda", gathered[1:4], mix_square[0], precision=PRECISE)
    tensors = jnp.einsum("mca,cd->mda", gathered[4:9], mix_square[1], precision=PRECISE)
    scalars = scalar_prev + jax.nn.silu(mixed[:channels])
    vectors = jax.nn.sigmoid(mixed[channels : 2 * channels])[None] * vectors
    tensors = jax.nn.sigmoid(mixed[2 * channels :])[None] * tensors
    return jnp.concatenate([scalars[None], vectors, tensors], axis=0)


def second_messages(
    first_harm, second_harm, bessel, sender_feat, edge_weight, weight_in, weight_out
):
    channels = sender_feat.shape[1]
    edge_weights = radial(bessel, weight_in, weight_out)
    along_first = jnp.einsum("kce,ke->ce", sender_feat[1:4], first_harm, precision=PRECISE)
    along_second = jnp.einsum("kce,ke->ce", sender_feat[4:9], second_harm, precision=PRECISE)
    combined = (
        edge_weights[:channels] * sender_feat[0]
        + edge_weights[channels : 2 * channels] * along_first
        + edge_weights[2 * channels :] * along_second
    )
    return combined * edge_weight


def node_second(features, summed, mix_square, readout):
    scalars = features[0] + jax.nn.silu(
        jnp.einsum("cd,ca->da", mix_square[2], summed * INV_NEIGH, precision=PRECISE)
    )
    return jnp.einsum("c,ca->a", readout, scalars, precision=PRECISE)


def factored(gradient, weight, row_state, col_state):
    decay_rate = 1.0 - STEP_NUM ** (-0.8)
    squares = gradient * gradient + EPS_SQUARE
    row_new = decay_rate * row_state + (1.0 - decay_rate) * jnp.mean(squares, axis=-1)
    col_new = decay_rate * col_state + (1.0 - decay_rate) * jnp.mean(squares, axis=-2)
    second = (
        row_new[..., :, None]
        * col_new[..., None, :]
        / jnp.mean(row_new, axis=-1, keepdims=True)[..., None]
    )
    weight_rms = jnp.sqrt(jnp.mean(weight * weight, axis=(-2, -1), keepdims=True) + 1e-06)
    weight_new = weight - RELATIVE * weight_rms * gradient * lax.rsqrt(second)
    return (gradient, row_new, col_new, weight_new, weight_new.astype(jnp.bfloat16))


def unfactored(gradient, weight, second):
    decay_rate = 1.0 - STEP_NUM ** (-0.8)
    second_new = decay_rate * second + (1.0 - decay_rate) * (gradient * gradient + EPS_SQUARE)
    weight_rms = jnp.sqrt(jnp.mean(weight * weight) + 1e-06)
    weight_new = weight - RELATIVE * weight_rms * gradient * lax.rsqrt(second_new)
    return (gradient, second_new, weight_new, weight_new.astype(jnp.bfloat16))


def add_trees(trees):
    return reduce(lambda left, right: jax.tree.map(jnp.add, left, right), trees)


def per_system(values):
    return values.reshape(SYS_LOC, -1).sum(axis=1)


def build(send_row, arrived_lists, mask_row, atom_count, spec_hot):
    edge_weight = mask_row.astype(jnp.float32)
    arrived_row = arrived_lists[0]
    send_hot = (send_row[None, :] == jnp.arange(atom_count)[:, None]).astype(jnp.float32)
    inc_hot = (arrived_row[None, :] == jnp.arange(atom_count)[:, None]).astype(jnp.float32)

    def fetch_positions(coords):
        return lax.all_to_all(
            jnp.dot(coords, inc_hot, precision=PRECISE),
            "edge",
            split_axis=1,
            concat_axis=1,
            tiled=True,
        )

    def return_positions(cotangent):
        arrived = lax.all_to_all(cotangent, "edge", split_axis=1, concat_axis=1, tiled=True)
        return jnp.einsum("de,ae->da", arrived, inc_hot, precision=PRECISE)

    def collect(values):
        arrived = lax.all_to_all(values, "edge", split_axis=2, concat_axis=2, tiled=True)
        return jnp.einsum("mce,ae->mca", arrived, inc_hot, precision=PRECISE)

    def spread(values):
        per_slot = jnp.einsum("mca,ae->mce", values, inc_hot, precision=PRECISE)
        return lax.all_to_all(per_slot, "edge", split_axis=2, concat_axis=2, tiled=True)

    def scalar_start(params):
        return jnp.einsum("tc,ta->ca", params[0], spec_hot, precision=PRECISE)

    def give_back(aux_cot, recv_cot):
        return return_positions(aux_cot + recv_cot)

    def edge_first(coords, recv_pos, params):
        first_harm, second_harm, bessel = geometry(
            jnp.dot(coords, send_hot, precision=PRECISE), recv_pos
        )
        sender_feat = jnp.dot(scalar_start(params), send_hot, precision=PRECISE)
        return first_messages(
            first_harm, second_harm, bessel, sender_feat, edge_weight, params[1][0], params[2][0]
        )

    def collect_first(values):
        return collect(values)

    def spread_first(values):
        return spread(values)

    def node_one(summed, params):
        return node_first(summed, scalar_start(params), params[3], params[4])

    def edge_second(coords, recv_pos, features, params):
        first_harm, second_harm, bessel = geometry(
            jnp.dot(coords, send_hot, precision=PRECISE), recv_pos
        )
        sender_feat = jnp.einsum("mca,ae->mce", features, send_hot, precision=PRECISE)
        return second_messages(
            first_harm, second_harm, bessel, sender_feat, edge_weight, params[1][1], params[2][1]
        )[None]

    def node_two(features, summed, params):
        return node_second(features, summed[0], params[4], params[5])

    def back_node_two(features, summed, params):
        _, pullback = jax.vjp(
            lambda feature_in, summed_in: node_two(feature_in, summed_in, params), features, summed
        )
        return pullback(jnp.ones((atom_count,), jnp.float32))

    def back_edge_two(coords, recv_pos, features, params, cotangent):
        _, pullback = jax.vjp(
            lambda where_at, recv_at, feature_in: edge_second(
                where_at, recv_at, feature_in, params
            ),
            coords,
            recv_pos,
            features,
        )
        return pullback(cotangent)

    def back_node_one(summed, params, cotangent):
        _, pullback = jax.vjp(lambda summed_in: node_one(summed_in, params), summed)
        return pullback(cotangent)[0]

    def back_edge_one(coords, aux_pos, params, cotangent):
        _, pullback = jax.vjp(
            lambda where_at, aux_at: edge_first(where_at, aux_at, params), coords, aux_pos
        )
        return pullback(cotangent)

    def evaluate(coords, params):
        recv_pos = fetch_positions(coords)
        summed_one = collect_first(edge_first(coords, recv_pos, params))
        features = node_one(summed_one, params)
        summed_two = collect(edge_second(coords, recv_pos, features, params))
        energies = node_two(features, summed_two, params)
        feature_node, summed_two_bar = back_node_two(features, summed_two, params)
        second_bar = spread(summed_two_bar)
        coord_second, recv_second, feature_edge = back_edge_two(
            coords, recv_pos, features, params, second_bar
        )
        feature_bar = feature_node + feature_edge
        first_bar = spread_first(back_node_one(summed_one, params, feature_bar))
        coord_first, aux_first = back_edge_one(coords, recv_pos, params, first_bar)
        forces = -(coord_first + coord_second + give_back(aux_first, recv_second))
        stored = (
            coords,
            recv_pos,
            recv_pos,
            summed_one,
            features,
            summed_two,
            second_bar,
            feature_bar,
            first_bar,
        )
        return (energies, forces, stored)

    def reverse(stored, params, energy_bar, force_bar):
        (
            coords,
            recv_pos,
            aux_pos,
            summed_one,
            features,
            summed_two,
            second_bar,
            feature_bar,
            first_bar,
        ) = stored
        coord_cot = -force_bar
        recv_cot = fetch_positions(coord_cot)
        _, pullback = jax.vjp(back_edge_one, coords, aux_pos, params, first_bar)
        coord_one, aux_one, param_one, first_cot = pullback((coord_cot, recv_cot))
        _, pullback = jax.vjp(back_node_one, summed_one, params, feature_bar)
        summed_one_a, param_two, feature_cot = pullback(collect_first(first_cot))
        _, pullback = jax.vjp(back_edge_two, coords, recv_pos, features, params, second_bar)
        coord_two, recv_two, feature_one, param_three, second_cot = pullback(
            (coord_cot, recv_cot, feature_cot)
        )
        _, pullback = jax.vjp(back_node_two, features, summed_two, params)
        feature_two, summed_two_a, param_four = pullback((feature_cot, collect(second_cot)))
        _, pullback = jax.vjp(node_two, features, summed_two, params)
        feature_three, summed_two_b, param_five = pullback(energy_bar)
        _, pullback = jax.vjp(edge_second, coords, recv_pos, features, params)
        coord_three, recv_three, feature_four, param_six = pullback(
            spread(summed_two_a + summed_two_b)
        )
        _, pullback = jax.vjp(node_one, summed_one, params)
        summed_one_b, param_seven = pullback(
            feature_one + feature_two + feature_three + feature_four
        )
        _, pullback = jax.vjp(edge_first, coords, aux_pos, params)
        coord_four, aux_four, param_eight = pullback(spread_first(summed_one_a + summed_one_b))
        coord_total = (
            coord_one
            + coord_two
            + coord_three
            + coord_four
            + give_back(aux_one + aux_four, recv_two + recv_three)
        )
        param_total = add_trees(
            [
                param_one,
                param_two,
                param_three,
                param_four,
                param_five,
                param_six,
                param_seven,
                param_eight,
            ]
        )
        return (coord_total, param_total)

    return (evaluate, reverse)


def update(summed, params, states):
    embedding, radial_in, radial_out, mix_first, mix_square, readout = params
    (
        embedding_rows,
        embedding_cols,
        radial_in_rows,
        radial_in_cols,
        radial_out_rows,
        radial_out_cols,
        mix_first_rows,
        mix_first_cols,
        mix_square_rows,
        mix_square_cols,
        readout_second,
    ) = states
    emb = factored(summed[0], embedding, embedding_rows, embedding_cols)
    rin = factored(summed[1], radial_in, radial_in_rows, radial_in_cols)
    rout = factored(summed[2], radial_out, radial_out_rows, radial_out_cols)
    mfirst = factored(summed[3], mix_first, mix_first_rows, mix_first_cols)
    msquare = factored(summed[4], mix_square, mix_square_rows, mix_square_cols)
    rdout = unfactored(summed[5], readout, readout_second)
    return (
        summed[6],
        emb[0],
        emb[1],
        emb[2],
        emb[3],
        emb[4],
        rin[0],
        rin[1],
        rin[2],
        rin[3],
        rin[4],
        rout[0],
        rout[1],
        rout[2],
        rout[3],
        rout[4],
        mfirst[0],
        mfirst[1],
        mfirst[2],
        mfirst[3],
        mfirst[4],
        msquare[0],
        msquare[1],
        msquare[2],
        msquare[3],
        msquare[4],
        rdout[0],
        rdout[1],
        rdout[2],
        rdout[3],
    )


F32 = jnp.float32
BF = jnp.bfloat16
MESH = pl.DeviceIdType.MESH
ROOT15 = math.sqrt(15.0)
TILES = 2
CHUNK = 16
LANES_AT_ONCE = 256
N_COMP = 9
PATHS = ((0, 3, 0), (3, 8, 1))
KIND_INIT, KIND_EDGES, KIND_MSG, KIND_COT, KIND_FORCE = 0, 1, 2, 3, 4
KIND_TMSG, KIND_TCOT, KIND_TFORCE, KIND_SCATTER, KIND_GATHER, KIND_SYS = 5, 6, 7, 8, 9, 10
KIND_OWN, KIND_SCATTER_LATE = 11, 12
KINDS = 13


def dot_nn(left, right):
    return lax.dot_general(left, right, (((1,), (0,)), ((), ())), preferred_element_type=F32)


def dot_nt(left, right):
    return lax.dot_general(left, right, (((1,), (1,)), ((), ())), preferred_element_type=F32)


def two_parts(value):
    high = value.astype(BF)
    return high, (value - high.astype(F32)).astype(BF)


def two_parts_f32(value):
    high = value.astype(BF).astype(F32)
    return high, value - high


def three_parts_f32(value):
    high = value.astype(BF).astype(F32)
    rest = value - high
    middle = rest.astype(BF).astype(F32)
    return high, middle, rest - middle


def left_three(weight):
    high, low = two_parts_f32(weight)
    return jnp.concatenate([high, high, low], axis=1).astype(BF)


def right_three(value):
    high, low = two_parts(value)
    return jnp.concatenate([high, low, high], axis=0)


def right_three_small(value):
    high, low = two_parts_f32(value)
    return jnp.concatenate([high, low, high, jnp.zeros_like(high)], axis=0).astype(BF)


def stack_three(value):
    high, middle, low = three_parts_f32(value)
    return jnp.concatenate([high, middle, low, jnp.zeros_like(high)], axis=0).astype(BF)


def join_three(value):
    return value[0:8] + value[8:16] + value[16:24]


def outer_three(left, right):
    left_high, left_low = two_parts(left)
    right_high, right_low = two_parts(right)
    return (
        dot_nt(left_high, right_high)
        + dot_nt(left_low, right_high)
        + dot_nt(left_high, right_low)
    )


def logistic(value):
    return 1.0 / (1.0 + jnp.exp(jnp.minimum(-value, 80.0)))


def silu_slope(value, gate):
    return gate * (1.0 + value * (1.0 - gate))


def silu_bend(value, gate):
    return gate * (1.0 - gate) * (2.0 + value * (1.0 - 2.0 * gate))


def sin_cos_pi(turns):
    whole = jnp.floor(turns + 0.5)
    part = turns - whole
    sign = 1.0 - 2.0 * (whole - 2.0 * jnp.floor(0.5 * whole))
    square = part * part
    sine = 0.0
    for order in range(15, 0, -2):
        sine = sine * square + (-1.0) ** (order // 2) * math.pi**order / math.factorial(order)
    cosine = 0.0
    for order in range(16, -1, -2):
        cosine = cosine * square + (-1.0) ** (order // 2) * math.pi**order / math.factorial(order)
    return sign * (part * sine), sign * cosine


def sin_cos_multiples(sine, cosine):
    sines, cosines = [None, sine], [None, cosine]
    for order in range(2, 9):
        half, rest = order // 2, order - order // 2
        sines.append(sines[half] * cosines[rest] + cosines[half] * sines[rest])
        cosines.append(cosines[half] * cosines[rest] - sines[half] * sines[rest])
    return sines[1:], cosines[1:]


def second_slope(one, two, three, given):
    return (
        ROOT15 * (two * given[0] + three * given[3] + one * given[4]),
        ROOT15 * (one * given[0] + three * given[1] - two * given[4]),
        ROOT15 * (two * given[1] + one * given[3]) + 3.0 * ROOT5 * three * given[2],
    )


def rows_of(value, first, count):
    return [value[first + number : first + number + 1] for number in range(count)]


def step_kernel(
    n_edge,
    n_sys,
    pos_ref,
    vel_ref,
    spec_ref,
    send_ref,
    recv_ref,
    mask_ref,
    emb_ref,
    rin_ref,
    rout_ref,
    mfirst_ref,
    msquare_ref,
    readout_ref,
    total_ref,
    scratch,
):
    s = scratch
    channels = emb_ref.shape[1]
    wide = N_COMP * channels
    atoms = pos_ref.shape[1]
    tiles = TILES
    group = n_edge // tiles
    lanes = group * atoms
    chunks = channels // CHUNK
    held_group = lax.axis_index("sys")
    held_part = lax.axis_index("edge")
    my_group = lax.div(held_part, 2)
    core = lax.rem(held_part, 2)
    me = 2 * held_group + core
    half = lax.div(me, group)
    half_atoms = atoms // SYS_LOC

    def peer(distance):
        return jnp.bitwise_xor(me, distance)

    def place_of(which_group, part):
        return {"sys": lax.div(part, 2), "edge": 2 * which_group + lax.rem(part, 2)}

    def remote(source, target, kind, other):
        return pltpu.make_async_remote_copy(
            src_ref=source,
            dst_ref=target,
            send_sem=s.send_sem.at[kind, other],
            recv_sem=s.recv_sem.at[kind, me],
            device_id=place_of(my_group, other),
            device_id_type=MESH,
        )

    def landed(target, kind, other):
        pltpu.make_async_remote_copy(
            src_ref=target,
            dst_ref=target,
            send_sem=s.send_sem.at[kind, other],
            recv_sem=s.recv_sem.at[kind, other],
            device_id=place_of(my_group, other),
            device_id_type=MESH,
        ).wait_recv()

    def each_peer(action):
        def body(distance, carry):
            action(peer(distance))
            return carry

        lax.fori_loop(1, n_edge, body, 0)

    def each_tile(action):
        for index in range(tiles):
            action(index)

    def loop(count, action, unroll=False):
        def body(index, carry):
            action(index)
            return carry

        lax.fori_loop(0, count, body, 0, unroll=unroll)

    def chunk_at(base, index):
        return slice(base + index * CHUNK, base + (index + 1) * CHUNK)

    barrier = pltpu.get_barrier_semaphore()

    def greet(device):
        pl.semaphore_signal(barrier, inc=1, device_id=device, device_id_type=MESH)

    stays = held_group == my_group

    def each_given(action):
        def body(part, carry):
            @pl.when(jnp.logical_not(jnp.logical_and(stays, part == held_part)))
            def _():
                action(part)

            return carry

        lax.fori_loop(0, n_edge, body, 0)

    def each_group(action):
        def body(distance, carry):
            action(lax.rem(my_group + distance, n_sys))
            return carry

        lax.fori_loop(1, n_sys, body, 0)

    each_given(lambda part: greet({"sys": my_group, "edge": part}))
    each_peer(lambda other: greet(place_of(my_group, other)))
    each_group(lambda other: greet({"edge": 2 * other + core}))

    s.start_out[...] = jnp.concatenate([pos_ref[...], vel_ref[...], pos_ref[0:2]], axis=0)
    species_rows = jnp.broadcast_to(spec_ref[...].reshape(1, atoms), (16 - 3 * EVALS, atoms))
    for other in range(n_edge):
        at = slice(other * atoms, (other + 1) * atoms)
        for part, ref in enumerate((send_ref, recv_ref, mask_ref)):
            s.lists_out[other, part * EVALS : (part + 1) * EVALS, :] = ref[:, at]
        s.lists_out[other, 3 * EVALS :, :] = species_rows

    pl.semaphore_wait(barrier, 2 * n_edge - 1 + n_sys - 1 - jnp.where(stays, 1, 0))

    def given(source, target, kind, part):
        return pltpu.make_async_remote_copy(
            src_ref=source,
            dst_ref=target,
            send_sem=s.send_sem.at[kind, part],
            recv_sem=s.recv_sem.at[kind, held_part],
            device_id=place_of(held_group, part),
            device_id_type=MESH,
        )

    def taken(target, kind, part):
        pltpu.make_async_remote_copy(
            src_ref=target,
            dst_ref=target,
            send_sem=s.send_sem.at[kind, part],
            recv_sem=s.recv_sem.at[kind, part],
            device_id={"sys": my_group, "edge": part},
            device_id_type=MESH,
        ).wait_recv()

    def give_atoms(part):
        return given(s.start_out, s.start_float.at[held_part], KIND_INIT, part)

    def give_slots(part):
        return given(s.lists_out.at[part], s.lists_in.at[held_part], KIND_EDGES, part)

    def give_lists():
        return given(s.lists_out, s.lists_own, KIND_OWN, held_part)

    def start_first(part):
        give_atoms(part).start()
        give_slots(part).start()

    each_given(start_first)

    @pl.when(jnp.logical_not(stays))
    def _():
        give_lists().start()

    @pl.when(stays)
    def _():
        s.start_float[me] = s.start_out[...]
        s.lists_in[me] = s.lists_out[me]
        s.lists_own[...] = s.lists_out[...]

    for layer in range(2):
        w_in = rin_ref[layer]
        high, low = two_parts_f32(w_in)
        zero = jnp.zeros_like(high)
        s.w_in_left[layer] = jnp.concatenate([high, high, low, zero], axis=0).T.astype(BF)
        s.w_in_back[layer] = jnp.concatenate(
            [
                jnp.concatenate([high, high], axis=1),
                jnp.concatenate([low, zero], axis=1),
            ],
            axis=0,
        ).astype(BF)
        w_out = rout_ref[layer]
        s.w_out_left[layer] = left_three(w_out.T)
        s.w_out_back[layer] = jnp.concatenate(two_parts_f32(w_out), axis=0).astype(BF)
    s.mf_left[...] = left_three(mfirst_ref[...].T)
    s.mf_back[...] = left_three(mfirst_ref[...])
    for number in range(3):
        s.ms_left[number] = left_three(msquare_ref[number].T)
        s.ms_back[number] = left_three(msquare_ref[number])
    emb_pad = jnp.concatenate(
        [emb_ref[...], jnp.zeros((16 - emb_ref.shape[0], channels), F32)], axis=0
    )
    s.emb_left[...] = jnp.concatenate(list(three_parts_f32(emb_pad)), axis=0).T.astype(BF)
    s.readout_col[...] = jnp.broadcast_to(
        readout_ref[...].reshape(1, channels), (atoms, channels)
    ).T
    for ref in (
        s.grad_emb,
        s.grad_in,
        s.grad_out,
        s.grad_mf,
        s.grad_ms,
        s.grad_ro,
        s.grad_second,
        s.grad_first,
    ):
        ref[...] = jnp.zeros_like(ref)

    def first_landed(part):
        taken(s.start_float.at[part], KIND_INIT, part)
        taken(s.lists_in.at[part], KIND_EDGES, part)

    each_given(first_landed)

    @pl.when(jnp.logical_not(stays))
    def _():
        taken(s.lists_own, KIND_OWN, me)

    def first_sent(part):
        give_atoms(part).wait_send()
        give_slots(part).wait_send()

    each_given(first_sent)

    @pl.when(jnp.logical_not(stays))
    def _():
        give_lists().wait_send()

    def species_values(hot):
        return dot_nn(s.emb_left[...], jnp.concatenate([hot, hot, hot], axis=0))

    own_species = s.lists_in[me, 3 * EVALS : 3 * EVALS + 1, :]
    own_species = lax.broadcasted_iota(jnp.int32, (16, atoms), 0) == own_species
    s.own_kind[...] = own_species.astype(F32).astype(BF)
    s.start_scalar[...] = species_values(s.own_kind[...])
    s.rows[...] = jnp.zeros_like(s.rows)
    for axis in range(3):
        s.place[axis] = s.start_float[:, axis, :]
        s.speed[axis] = s.start_float[:, 3 + axis, :]

    def one_hots(number):
        atom_row = lax.broadcasted_iota(jnp.int32, (atoms, atoms), 0)

        def hot(row):
            return (atom_row == row).astype(F32).astype(BF)

        def put_own(tile, at, value):
            s.own_hot[number, tile, 0:atoms, at] = value
            s.own_hot[number, tile, atoms:, at] = value

        def body(index):
            for part in range(group):
                other = index * group + part
                at = pl.ds(part * atoms, atoms)
                out_list = s.lists_own.at[other]
                in_list = s.lists_in.at[other]
                sender = out_list[pl.ds(number, 1), :]
                receiver = out_list[pl.ds(EVALS + number, 1), :]
                mask = out_list[pl.ds(2 * EVALS + number, 1), :]
                put_own(index, at, hot(sender))
                s.far_hot[number, index, :, at] = hot(jnp.where(mask == 0, -1, receiver))
                sender = in_list[pl.ds(number, 1), :]
                receiver = in_list[pl.ds(EVALS + number, 1), :]
                mask = in_list[pl.ds(2 * EVALS + number, 1), :]
                sender_hot = hot(sender)
                put_own(tiles + index, at, hot(jnp.where(mask == 0, -1, receiver)))
                s.far_hot[number, tiles + index, :, at] = sender_hot
                species = in_list[pl.ds(3 * EVALS, 1), :]
                kinds = lax.broadcasted_iota(jnp.int32, (16, atoms), 0)
                species_hot = (kinds == species).astype(F32).astype(BF)
                s.kind_hot[number, index, :, at] = dot_nn(species_hot, sender_hot).astype(BF)
            s.kind_value[number, index] = species_values(s.kind_hot[number, index])

        each_tile(body)

    def table(rows):
        for axis in range(3):
            s.rows[:, axis, :] = rows[axis]
        for other in range(n_edge):
            s.pieces[other] = stack_three(s.rows[other])

    def edge_difference(number, index):
        sign = jnp.where(index < tiles, 1.0, -1.0)
        own = dot_nn(s.pieces[me], s.own_hot[number, index, 0:atoms, :])
        first = lax.rem(index, tiles) * group
        far = [
            dot_nn(
                s.pieces[first + part],
                s.far_hot[number, index, :, part * atoms : (part + 1) * atoms],
            )
            for part in range(group)
        ]
        return sign * join_three(own - jnp.concatenate(far, axis=1))

    def scatter_rows(number, target):
        parts = [stack_three(s.edge_rows[index]) for index in range(2 * tiles)]
        own = 0.0
        for index in range(2 * tiles):
            found = dot_nt(parts[index], s.own_hot[number, index, 0:atoms, :])
            own = own + found if index < tiles else own - found
        s.row_own[...] = join_three(own)
        for other in range(n_edge):
            index, part = other // group, other % group
            at = slice(part * atoms, (part + 1) * atoms)
            total = join_three(
                dot_nt(parts[tiles + index][:, at], s.far_hot[number, tiles + index, :, at])
                - dot_nt(parts[index][:, at], s.far_hot[number, index, :, at])
            )
            for axis in range(3):
                target[axis, other : other + 1, :] = total[axis : axis + 1]
        for axis in range(3):
            target[axis, pl.ds(me, 1), :] += s.row_own[axis : axis + 1, :]

    def geometry(number, index):
        offset = edge_difference(number, index)
        geo = s.geo.at[number, index]
        radius = jnp.sqrt(jnp.sum(offset * offset, axis=0, keepdims=True) + SOFTEN)
        inverse = 1.0 / radius
        unit = offset * inverse
        one, two, three = rows_of(unit, 0, 3)
        geo[0:3, :] = ROOT3 * unit[0:3]
        geo[3:4, :] = ROOT15 * one * two
        geo[4:5, :] = ROOT15 * two * three
        geo[5:6, :] = 0.5 * ROOT5 * (3.0 * three * three - 1.0)
        geo[6:7, :] = ROOT15 * one * three
        geo[7:8, :] = 0.5 * ROOT15 * (one * one - two * two)
        t = radius * (1.0 / CUTOFF)
        sines, cosines = sin_cos_multiples(*sin_cos_pi(t))
        sines = jnp.concatenate(sines, axis=0)
        cosines = jnp.concatenate(cosines, axis=0)
        t2 = t * t
        t4 = t2 * t2
        amount = math.sqrt(2.0 / CUTOFF) * inverse
        env = 1.0 - t4 * t2 * (28.0 - 48.0 * t + 21.0 * t2)
        env_one = -168.0 / CUTOFF * t4 * t * (1.0 - t) * (1.0 - t)
        env_two = -168.0 / CUTOFF**2 * t4 * (1.0 - t) * (5.0 - 7.0 * t)
        front = amount * env
        front_one = amount * (env_one - env * inverse)
        front_two = amount * (env_two - 2.0 * inverse * (env_one - env * inverse))
        waves = (lax.broadcasted_iota(jnp.int32, (NB, 1), 0) + 1).astype(F32) * (
            math.pi / CUTOFF
        )
        geo[8:16, :] = front * sines
        geo[16:24, :] = front_one * sines + front * waves * cosines
        geo[24:32, :] = (
            front_two * sines + 2.0 * front_one * waves * cosines - front * waves * waves * sines
        )
        geo[32:35, :] = unit[0:3]
        geo[35:36, :] = inverse

    def first_back(number, index):
        geo = s.geo.at[number, index]
        bars = s.geo_bar.at[number, index]
        ybar = rows_of(bars[0:8, :], 0, 8)
        slope = jnp.sum(bars[8:16, :] * geo[16:24, :], axis=0, keepdims=True)
        units = rows_of(geo[32:40, :], 0, 3)
        inverse = geo[35:36, :]
        extra = second_slope(*units, ybar[3:])
        back = [ROOT3 * ybar[axis] + extra[axis] for axis in range(3)]
        along = back[0] * units[0] + back[1] * units[1] + back[2] * units[2]
        rest = slope - along * inverse
        for axis in range(3):
            bars[16 + axis : 17 + axis, :] = back[axis]
            s.edge_rows[index, axis : axis + 1, :] = back[axis] * inverse + rest * units[axis]
        bars[19:20, :] = rest

    def geometry_tangent(number, index):
        move = edge_difference(number, index)
        geo = s.geo.at[number, index]
        out = s.geo_dot.at[index]
        inverse = geo[35:36, :]
        one, two, three = rows_of(geo[32:40, :], 0, 3)
        moves = rows_of(move, 0, 3)
        speed = one * moves[0] + two * moves[1] + three * moves[2]
        d_one, d_two, d_three = [
            (amount - unit * speed) * inverse for amount, unit in zip(moves, (one, two, three))
        ]
        out[0:1, :] = ROOT3 * d_one
        out[1:2, :] = ROOT3 * d_two
        out[2:3, :] = ROOT3 * d_three
        out[3:4, :] = ROOT15 * (d_one * two + one * d_two)
        out[4:5, :] = ROOT15 * (d_two * three + two * d_three)
        out[5:6, :] = 3.0 * ROOT5 * three * d_three
        out[6:7, :] = ROOT15 * (d_one * three + one * d_three)
        out[7:8, :] = ROOT15 * (one * d_one - two * d_two)
        out[8:16, :] = geo[16:24, :] * speed
        out[16:17, :] = d_one
        out[17:18, :] = d_two
        out[18:19, :] = d_three
        out[19:20, :] = speed
        out[20:23, :] = move[0:3]

    def second_back(number, index, hats):
        geo = s.geo.at[number, index]
        bars = s.geo_bar.at[number, index]
        dots = s.geo_dot.at[index]
        units = rows_of(geo[32:40, :], 0, 3)
        inverse = geo[35:36, :]
        turns = rows_of(dots[16:24, :], 0, 3)
        speed = dots[19:20, :]
        moves = rows_of(dots[16:24, :], 4, 3)
        back = rows_of(bars[16:24, :], 0, 3)
        rest = bars[19:20, :]
        yhat = rows_of(hats, 0, 8)
        ybar = rows_of(bars[0:8, :], 0, 8)
        extra = second_slope(*units, yhat[3:])
        more = second_slope(*turns, ybar[3:])
        radial_hat = jnp.sum(
            hats[8:16] * geo[16:24, :] + speed * (bars[8:16, :] * geo[24:32, :]),
            axis=0,
            keepdims=True,
        ) - inverse * (turns[0] * back[0] + turns[1] * back[1] + turns[2] * back[2])
        unit_hat = [
            ROOT3 * yhat[axis]
            + extra[axis]
            + more[axis]
            - speed * inverse * back[axis]
            + rest * moves[axis]
            for axis in range(3)
        ]
        along = unit_hat[0] * units[0] + unit_hat[1] * units[1] + unit_hat[2] * units[2]
        left = radial_hat - along * inverse
        for axis in range(3):
            s.edge_rows[index, axis : axis + 1, :] = unit_hat[axis] * inverse + left * units[axis]

    def radial_forward(layer, number, index, basis):
        before = dot_nn(s.w_in_left[layer], right_three_small(basis))
        s.hidden[layer, number, index] = before
        gate = logistic(before)
        s.radial[layer, number, index] = dot_nn(
            s.w_out_left[layer], right_three(before * gate)
        )

    def radial_tangent(layer, number, index, basis_dot):
        before = s.hidden[layer, number, index]
        before_dot = dot_nn(s.w_in_left[layer], right_three_small(basis_dot))
        s.hidden_dot[layer, index] = before_dot
        gate = logistic(before)
        s.radial_dot[layer, index] = dot_nn(
            s.w_out_left[layer], right_three(silu_slope(before, gate) * before_dot)
        )

    def rows_pair(value):
        return jnp.concatenate(two_parts(value), axis=0)

    def hidden_back(layer, pair):
        half_rows = 3 * channels
        left = s.w_out_back[layer]
        found = dot_nn(left, pair[0:half_rows])
        return found[0:channels] + found[channels:] + dot_nn(left[0:channels], pair[half_rows:])

    def basis_back(layer, pair):
        found = dot_nn(s.w_in_back[layer], pair)
        return found[0:8] + found[8:16]

    def radial_back(layer, number, index):
        hidden_bar = hidden_back(layer, s.r_pair[layer, index])
        s.hidden_bar[layer, number, index] = hidden_bar
        before = s.hidden[layer, number, index]
        before_bar = silu_slope(before, logistic(before)) * hidden_bar
        return basis_back(layer, rows_pair(before_bar))

    def radial_second(layer, number, index, last):
        hidden_hat = hidden_back(layer, s.h_pair[layer, index])
        before = s.hidden[layer, number, index]
        before_dot = s.hidden_dot[layer, index]
        hidden_bar = s.hidden_bar[layer, number, index]
        gate = logistic(before)
        slope = silu_slope(before, gate)
        before_hat = slope * hidden_hat + silu_bend(before, gate) * before_dot * hidden_bar
        s.out_pair[layer, index] = rows_pair(before * gate)
        hat_pair = rows_pair(before_hat)
        s.hat_pair[layer, index] = hat_pair
        return None if last else basis_back(layer, hat_pair)

    def radial_gradients(layer, number):
        for index in range(tiles):
            s.grad_out[layer] += dot_nt(s.h_pair[layer, index], s.out_pair[layer, index])
            tile = index if layer == 1 else tiles + index
            basis = jnp.concatenate(two_parts_f32(s.geo[number, tile, 8:16, :]), axis=0)
            s.grad_in[layer] += dot_nt(basis.astype(BF), s.hat_pair[layer, index])

    def early_gradients(layer, number, index):
        before = s.hidden[layer, number, index]
        slope = silu_slope(before, logistic(before))
        dot_pair = rows_pair(slope * s.hidden_dot[layer, index])
        bar_pair = rows_pair(slope * s.hidden_bar[layer, number, index])
        s.grad_out[layer] += dot_nt(s.r_pair[layer, index], dot_pair)
        tile = index if layer == 1 else tiles + index
        basis_dot = jnp.concatenate(two_parts_f32(s.geo_dot[tile, 8:16, :]), axis=0)
        s.grad_in[layer] += dot_nt(basis_dot.astype(BF), bar_pair)

    def first_early(number, index):
        geo = s.geo.at[number, tiles + index]
        cot = s.first_cot.at[number, index]
        kind = s.kind_value.at[number, index]

        def body(c, lane):
            value = kind[chunk_at(0, c), lane]
            y = harmonic_rows(geo, lane)
            put_pair(s.r_pair.at[0, index], 0, c, lane, cot[chunk_at(0, c), lane] * value)
            for first, last, path in ((0, 3, 1), (3, 8, 2)):
                total = 0.0
                for k in range(first, last):
                    total = total + cot[chunk_at((k + 1) * channels, c), lane] * y[k]
                put_pair(s.r_pair.at[0, index], path, c, lane, total * value)

        over_chunks(body)
        early_gradients(0, number, index)

    def second_early(number, index):
        cot = s.msg_cot.at[number, index]
        feat = s.feat.at[number, index]

        def body(c, lane):
            at = chunk_at(0, c)
            given = cot[at, lane]
            put_pair(s.r_pair.at[1, index], 0, c, lane, feat[at, lane] * given)
            for path in (1, 2):
                along = s.along[number, index, chunk_at((path - 1) * channels, c), lane]
                put_pair(s.r_pair.at[1, index], path, c, lane, along * given)

        over_chunks(body)
        early_gradients(1, number, index)

    def all_early(number):
        for index in range(tiles):
            second_early(number, index)
            first_early(number, index)
        for first, last, path in PATHS:
            bars = [s.raw_bar[number, k * channels : (k + 1) * channels, :] for k in range(first, last)]
            s.grad_ms[path] += outer_three(
                side_by_side(s.agg_dot, first, last), jnp.concatenate(bars, axis=1)
            )
        s.grad_mf[...] += outer_three(s.mixed_bar[number], part_of(s.agg_dot, 0))

    def kind_gradients(number):
        for index in range(tiles):
            kinds = s.kind_hot[number, index]
            s.grad_emb[...] += dot_nt(kinds, s.v_high[index]) + dot_nt(kinds, s.v_low[index])
        high, low = two_parts(s.scalar_hat[...])
        s.grad_emb[...] += dot_nt(s.own_kind[...], high) + dot_nt(s.own_kind[...], low)

    def node_gradients(number):
        agg = s.agg.at[number]
        for first, last, path in PATHS:
            hats = [s.raw_hat[k * channels : (k + 1) * channels, :] for k in range(first, last)]
            s.grad_ms[path] += outer_three(
                side_by_side(agg, first, last), jnp.concatenate(hats, axis=1)
            )
        s.grad_ms[2] += outer_three(s.agg_two[number], s.last_hat[...]) + outer_three(
            s.agg_two_dot[...], s.last_bar[...]
        )
        s.grad_mf[...] += outer_three(s.mixed_hat[...], part_of(agg, 0))

    def put_pieces(high_ref, low_ref, lane, at, value):
        high, low = two_parts(value)
        high_ref[at, lane] = high
        low_ref[at, lane] = low

    def put_pair(ref, path, c, lane, value):
        high, low = two_parts(value)
        ref[chunk_at(path * channels, c), lane] = high
        ref[chunk_at((3 + path) * channels, c), lane] = low

    def add_scatter(index, hot):
        s.sum_wide[...] += dot_nt(s.m_high[index], hot) + dot_nt(s.m_low[index], hot)

    def harmonic_rows(ref, lane):
        return [ref[row : row + 1, lane] for row in range(8)]

    def lane_parts():
        return [slice(first, first + LANES_AT_ONCE) for first in range(0, lanes, LANES_AT_ONCE)]

    def over_chunks(body):
        for lane in lane_parts():
            for c in range(chunks):
                body(c, lane)

    def over_chunks_sum(body):
        found = []
        for lane in lane_parts():
            sums = (0.0,) * 8
            for c in range(chunks):
                sums = body(c, lane, sums)
            found.append(sum_rows(sums))
        return jnp.concatenate(found, axis=1)

    def fold(value):
        return value[0:8] + value[8:16]

    def sum_rows(parts):
        if not hasattr(parts[0], "shape"):
            return jnp.zeros((8, LANES_AT_ONCE), F32)
        return jnp.concatenate([jnp.sum(part, axis=0, keepdims=True) for part in parts], axis=0)

    def first_forward(number, index):
        tile = tiles + index
        geo = s.geo.at[number, tile]
        radial_forward(0, number, index, geo[8:16, :])
        rad = s.radial.at[0, number, index]
        kind = s.kind_value.at[number, index]

        def body(c, lane):
            value = kind[chunk_at(0, c), lane]
            y = harmonic_rows(geo, lane)
            put_pieces(s.m_high.at[index], s.m_low.at[index], lane, chunk_at(0, c), rad[chunk_at(0, c), lane] * value)
            vector = rad[chunk_at(channels, c), lane] * value
            tensor = rad[chunk_at(2 * channels, c), lane] * value
            for k in range(8):
                part = (vector if k < 3 else tensor) * y[k]
                put_pieces(s.m_high.at[index], s.m_low.at[index], lane, chunk_at((k + 1) * channels, c), part)

        over_chunks(body)
        add_scatter(index, s.own_hot[number, tile, 0:atoms, :])

    def first_tangent(number, index):
        tile = tiles + index
        geo = s.geo.at[number, tile]
        dots = s.geo_dot.at[tile]
        radial_tangent(0, number, index, dots[8:16, :])
        rad = s.radial.at[0, number, index]
        rad_dot = s.radial_dot.at[0, index]
        kind = s.kind_value.at[number, index]

        def body(c, lane):
            value = kind[chunk_at(0, c), lane]
            y = harmonic_rows(geo, lane)
            y_dot = harmonic_rows(dots, lane)
            put_pieces(s.m_high.at[index], s.m_low.at[index], lane, chunk_at(0, c), rad_dot[chunk_at(0, c), lane] * value)
            vector = rad[chunk_at(channels, c), lane] * value
            tensor = rad[chunk_at(2 * channels, c), lane] * value
            vector_dot = rad_dot[chunk_at(channels, c), lane] * value
            tensor_dot = rad_dot[chunk_at(2 * channels, c), lane] * value
            for k in range(8):
                base, move = (vector, vector_dot) if k < 3 else (tensor, tensor_dot)
                part = move * y[k] + base * y_dot[k]
                put_pieces(s.m_high.at[index], s.m_low.at[index], lane, chunk_at((k + 1) * channels, c), part)

        over_chunks(body)
        add_scatter(index, s.own_hot[number, tile, 0:atoms, :])

    def gather_wide(hot):
        return dot_nn(s.a_pair[...], hot)

    def first_reverse(number, index):
        tile = tiles + index
        geo = s.geo.at[number, tile]
        s.first_cot[number, index] = gather_wide(s.own_hot[number, tile])
        cot = s.first_cot.at[number, index]
        rad = s.radial.at[0, number, index]
        kind = s.kind_value.at[number, index]

        def body(c, lane, sums):
            value = kind[chunk_at(0, c), lane]
            y = harmonic_rows(geo, lane)
            put_pair(s.r_pair.at[0, index], 0, c, lane, cot[chunk_at(0, c), lane] * value)
            sums = list(sums)
            for first, last, path in ((0, 3, 1), (3, 8, 2)):
                base = rad[chunk_at(path * channels, c), lane] * value
                total = 0.0
                for k in range(first, last):
                    given = cot[chunk_at((k + 1) * channels, c), lane]
                    total = total + given * y[k]
                    sums[k] = sums[k] + fold(base * given)
                put_pair(s.r_pair.at[0, index], path, c, lane, total * value)
            return tuple(sums)

        sums = over_chunks_sum(body)
        s.geo_bar[number, tile, 0:8, :] = sums
        s.geo_bar[number, tile, 8:16, :] = radial_back(0, number, index)
        first_back(number, tile)

    def first_second(number, index, final):
        tile = tiles + index
        geo = s.geo.at[number, tile]
        dots = s.geo_dot.at[tile]
        s.feat_dot[index] = gather_wide(s.own_hot[number, tile])
        hat = s.feat_dot.at[index]
        cot = s.first_cot.at[number, index]
        rad = s.radial.at[0, number, index]
        rad_dot = s.radial_dot.at[0, index]
        kind = s.kind_value.at[number, index]

        def body(c, lane, sums):
            value = kind[chunk_at(0, c), lane]
            y = harmonic_rows(geo, lane)
            y_dot = harmonic_rows(dots, lane)
            sums = list(sums)
            total = cot[chunk_at(0, c), lane]
            total_hat = hat[chunk_at(0, c), lane]
            put_pair(s.h_pair.at[0, index], 0, c, lane, total_hat * value)
            value_hat = rad[chunk_at(0, c), lane] * total_hat + rad_dot[chunk_at(0, c), lane] * total
            for first, last, path in ((0, 3, 1), (3, 8, 2)):
                rad_here = rad[chunk_at(path * channels, c), lane]
                rad_move = rad_dot[chunk_at(path * channels, c), lane]
                base = rad_here * value
                move = rad_move * value
                total = 0.0
                total_hat = 0.0
                for k in range(first, last):
                    given = cot[chunk_at((k + 1) * channels, c), lane]
                    given_hat = hat[chunk_at((k + 1) * channels, c), lane]
                    total = total + given * y[k]
                    total_hat = total_hat + (given_hat * y[k] + given * y_dot[k])
                    if not final:
                        sums[k] = sums[k] + fold(base * given_hat + move * given)
                put_pair(s.h_pair.at[0, index], path, c, lane, total_hat * value)
                value_hat = value_hat + rad_here * total_hat + rad_move * total
            put_pieces(s.v_high.at[index], s.v_low.at[index], lane, chunk_at(0, c), value_hat)
            return tuple(sums)

        sums = over_chunks_sum(body)
        basis_hat = radial_second(0, number, index, final)
        if not final:
            second_back(number, tile, jnp.concatenate([sums, basis_hat], axis=0))

    def gather_far(ref, number, index):
        found = []
        for part in range(group):
            pair = rows_pair(ref[index * group + part])
            here = dot_nn(pair, s.far_hot[number, index, :, part * atoms : (part + 1) * atoms])
            found.append(here[0:channels] + here[channels:])
        return jnp.concatenate(found, axis=1)

    def put_messages(number, index):
        for part in range(group):
            at = slice(part * atoms, (part + 1) * atoms)
            hot = s.far_hot[number, index, :, at]
            s.msg_out[index * group + part] = dot_nt(s.v_high[index, :, at], hot) + dot_nt(
                s.v_low[index, :, at], hot
            )

    def near_peer(distance):
        return half * group + jnp.bitwise_xor(lax.rem(me, group), distance)

    def far_peer(distance):
        return (1 - half) * group + jnp.bitwise_xor(lax.rem(me, group), group - 1 - distance)

    def message_to(other, kind):
        return remote(s.msg_out.at[other], s.msg_in.at[me], kind, other)

    def exchange_messages(number, kind, make):
        make(number, 1 - half)
        put_messages(number, 1 - half)
        for distance in range(group):
            message_to(far_peer(distance), kind).start()
        make(number, half)
        put_messages(number, half)
        for distance in range(group - 1, 0, -1):
            message_to(near_peer(distance), kind).start()

    def second_forward(number, index):
        geo = s.geo.at[number, index]
        radial_forward(1, number, index, geo[8:16, :])
        s.feat[number, index] = gather_wide(s.own_hot[number, index])
        feat = s.feat.at[number, index]
        rad = s.radial.at[1, number, index]

        def body(c, lane):
            y = harmonic_rows(geo, lane)
            total = rad[chunk_at(0, c), lane] * feat[chunk_at(0, c), lane]
            for first, last, path in ((0, 3, 1), (3, 8, 2)):
                along = 0.0
                for k in range(first, last):
                    along = along + feat[chunk_at((k + 1) * channels, c), lane] * y[k]
                s.along[number, index, chunk_at((path - 1) * channels, c), lane] = along
                total = total + rad[chunk_at(path * channels, c), lane] * along
            put_pieces(s.v_high.at[index], s.v_low.at[index], lane, chunk_at(0, c), total)

        over_chunks(body)

    def second_tangent(number, index):
        geo = s.geo.at[number, index]
        dots = s.geo_dot.at[index]
        radial_tangent(1, number, index, dots[8:16, :])
        s.feat_dot[index] = gather_wide(s.own_hot[number, index])
        feat = s.feat.at[number, index]
        feat_dot = s.feat_dot.at[index]
        rad = s.radial.at[1, number, index]
        rad_dot = s.radial_dot.at[1, index]

        def body(c, lane):
            y = harmonic_rows(geo, lane)
            y_dot = harmonic_rows(dots, lane)
            at = chunk_at(0, c)
            total = rad_dot[at, lane] * feat[at, lane] + rad[at, lane] * feat_dot[at, lane]
            for first, last, path in ((0, 3, 1), (3, 8, 2)):
                move = 0.0
                for k in range(first, last):
                    here = chunk_at((k + 1) * channels, c)
                    move = move + (feat_dot[here, lane] * y[k] + feat[here, lane] * y_dot[k])
                here = chunk_at((path - 1) * channels, c)
                s.along_dot[index, here, lane] = move
                here_rad = chunk_at(path * channels, c)
                total = total + (
                    rad_dot[here_rad, lane] * s.along[number, index, here, lane]
                    + rad[here_rad, lane] * move
                )
            put_pieces(s.v_high.at[index], s.v_low.at[index], lane, at, total)

        over_chunks(body)

    def second_reverse(number, index):
        geo = s.geo.at[number, index]
        s.msg_cot[number, index] = gather_far(s.cot_all, number, index)
        cot = s.msg_cot.at[number, index]
        feat = s.feat.at[number, index]
        rad = s.radial.at[1, number, index]

        def body(c, lane, sums):
            y = harmonic_rows(geo, lane)
            at = chunk_at(0, c)
            given = cot[at, lane]
            sums = list(sums)
            put_pair(s.r_pair.at[1, index], 0, c, lane, feat[at, lane] * given)
            put_pieces(s.m_high.at[index], s.m_low.at[index], lane, at, rad[at, lane] * given)
            for first, last, path in ((0, 3, 1), (3, 8, 2)):
                here = chunk_at(path * channels, c)
                along = s.along[number, index, chunk_at((path - 1) * channels, c), lane]
                put_pair(s.r_pair.at[1, index], path, c, lane, along * given)
                base = rad[here, lane] * given
                for k in range(first, last):
                    wide_at = chunk_at((k + 1) * channels, c)
                    put_pieces(s.m_high.at[index], s.m_low.at[index], lane, wide_at, base * y[k])
                    sums[k] = sums[k] + fold(base * feat[wide_at, lane])
            return tuple(sums)

        sums = over_chunks_sum(body)
        s.geo_bar[number, index, 0:8, :] = sums
        s.geo_bar[number, index, 8:16, :] = radial_back(1, number, index)
        first_back(number, index)
        add_scatter(index, s.own_hot[number, index, 0:atoms, :])

    def second_second(number, index, final):
        geo = s.geo.at[number, index]
        dots = s.geo_dot.at[index]
        s.msg_hat[index] = gather_far(s.cot_all, number, index)
        cot = s.msg_cot.at[number, index]
        feat = s.feat.at[number, index]
        feat_dot = s.feat_dot.at[index]
        rad = s.radial.at[1, number, index]
        rad_dot = s.radial_dot.at[1, index]

        def body(c, lane, sums):
            y = harmonic_rows(geo, lane)
            y_dot = harmonic_rows(dots, lane)
            at = chunk_at(0, c)
            given = cot[at, lane]
            given_hat = s.msg_hat[index, at, lane]
            sums = list(sums)
            put_pair(s.h_pair.at[1, index], 0, c, lane, feat[at, lane] * given_hat + feat_dot[at, lane] * given)
            put_pieces(s.m_high.at[index], s.m_low.at[index], lane, at, rad[at, lane] * given_hat + rad_dot[at, lane] * given)
            for first, last, path in ((0, 3, 1), (3, 8, 2)):
                here = chunk_at(path * channels, c)
                along_at = chunk_at((path - 1) * channels, c)
                along = s.along[number, index, along_at, lane]
                along_dot = s.along_dot[index, along_at, lane]
                put_pair(s.h_pair.at[1, index], path, c, lane, along * given_hat + along_dot * given)
                base = rad[here, lane] * given
                base_hat = rad[here, lane] * given_hat + rad_dot[here, lane] * given
                for k in range(first, last):
                    wide_at = chunk_at((k + 1) * channels, c)
                    put_pieces(s.m_high.at[index], s.m_low.at[index], lane, wide_at, base_hat * y[k] + base * y_dot[k])
                    if not final:
                        sums[k] = sums[k] + fold(
                            base_hat * feat[wide_at, lane] + base * feat_dot[wide_at, lane]
                        )
            return tuple(sums)

        sums = over_chunks_sum(body)
        basis_hat = radial_second(1, number, index, final)
        if not final:
            second_back(number, index, jnp.concatenate([sums, basis_hat], axis=0))
        add_scatter(index, s.own_hot[number, index, 0:atoms, :])

    def part_of(ref, component):
        return ref[component * channels : (component + 1) * channels, :]

    def side_by_side(ref, first, last):
        return jnp.concatenate([part_of(ref, k + 1) for k in range(first, last)], axis=1)

    def linear(left, value):
        return dot_nn(left, right_three(value))

    def keep_wide(component, value):
        high, low = two_parts(value)
        at = slice(component * channels, (component + 1) * channels)
        s.a_pair[at, 0:atoms] = high
        s.a_pair[at, atoms:] = low

    def node_first_forward(number):
        s.agg[number] = INV_NEIGH * s.sum_wide[...]
        agg = s.agg.at[number]
        mixed = linear(s.mf_left[...], part_of(agg, 0))
        s.mixed[number] = mixed
        before, gate_one, gate_two = [mixed[i * channels : (i + 1) * channels] for i in range(3)]
        scalar = s.start_scalar[...] + before * logistic(before)
        s.scalar[number] = scalar
        keep_wide(0, scalar)
        gates = (logistic(gate_one), logistic(gate_two))
        for first, last, path in PATHS:
            raws = linear(s.ms_left[path], side_by_side(agg, first, last))
            for k in range(first, last):
                raw = raws[:, (k - first) * atoms : (k - first + 1) * atoms]
                s.raw[number, k * channels : (k + 1) * channels, :] = raw
                keep_wide(k + 1, gates[path] * raw)

    def node_first_tangent(number):
        s.agg_dot[...] = INV_NEIGH * s.sum_wide[...]
        mixed = s.mixed.at[number]
        mixed_dot = linear(s.mf_left[...], part_of(s.agg_dot, 0))
        s.mixed_dot[...] = mixed_dot
        before = part_of(mixed, 0)
        scalar_dot = silu_slope(before, logistic(before)) * mixed_dot[0:channels]
        s.scalar_dot[...] = scalar_dot
        keep_wide(0, scalar_dot)
        for first, last, path in PATHS:
            gate = logistic(part_of(mixed, path + 1))
            move = gate * (1.0 - gate) * mixed_dot[(path + 1) * channels : (path + 2) * channels]
            raws_dot = linear(s.ms_left[path], side_by_side(s.agg_dot, first, last))
            for k in range(first, last):
                raw_dot = raws_dot[:, (k - first) * atoms : (k - first + 1) * atoms]
                s.raw_dot[k * channels : (k + 1) * channels, :] = raw_dot
                raw = s.raw[number, k * channels : (k + 1) * channels, :]
                keep_wide(k + 1, move * raw + gate * raw_dot)

    def node_first_reverse(number):
        s.feat_bar[number] = s.sum_wide[...]
        s.feat_bar[number, 0:channels, :] += s.readout_col[...]
        bar = s.feat_bar.at[number]
        mixed = s.mixed.at[number]
        before = part_of(mixed, 0)
        s.mixed_bar[number, 0:channels, :] = silu_slope(before, logistic(before)) * part_of(bar, 0)
        for first, last, path in PATHS:
            gate = logistic(part_of(mixed, path + 1))
            total = 0.0
            bars = []
            for k in range(first, last):
                given = part_of(bar, k + 1)
                total = total + given * s.raw[number, k * channels : (k + 1) * channels, :]
                raw_bar = gate * given
                s.raw_bar[number, k * channels : (k + 1) * channels, :] = raw_bar
                bars.append(raw_bar)
            found = INV_NEIGH * linear(s.ms_back[path], jnp.concatenate(bars, axis=1))
            for k in range(first, last):
                keep_wide(k + 1, found[:, (k - first) * atoms : (k - first + 1) * atoms])
            s.mixed_bar[number, (path + 1) * channels : (path + 2) * channels, :] = (
                gate * (1.0 - gate) * total
            )
        keep_wide(0, INV_NEIGH * linear(s.mf_back[...], s.mixed_bar[number]))

    def node_first_second(number, energy_bar):
        s.sum_wide[0:channels, :] += s.readout_col[...] * energy_bar
        hat = s.sum_wide
        bar = s.feat_bar.at[number]
        mixed = s.mixed.at[number]
        before = part_of(mixed, 0)
        gate = logistic(before)
        scalar_hat = part_of(hat, 0)
        s.mixed_hat[0:channels, :] = silu_slope(before, gate) * scalar_hat + silu_bend(
            before, gate
        ) * s.mixed_dot[0:channels, :] * part_of(bar, 0)
        s.scalar_hat[...] = scalar_hat
        for first, last, path in PATHS:
            gate = logistic(part_of(mixed, path + 1))
            slope = gate * (1.0 - gate)
            bend = slope * (1.0 - 2.0 * gate)
            mixed_dot = s.mixed_dot[(path + 1) * channels : (path + 2) * channels, :]
            one = 0.0
            two = 0.0
            hats = []
            for k in range(first, last):
                at = slice(k * channels, (k + 1) * channels)
                given = part_of(bar, k + 1)
                given_hat = part_of(hat, k + 1)
                raw = s.raw[number, at, :]
                one = one + (given_hat * raw + given * s.raw_dot[at, :])
                two = two + given * raw
                hats.append(gate * given_hat + slope * mixed_dot * given)
            for k in range(first, last):
                s.raw_hat[k * channels : (k + 1) * channels, :] = hats[k - first]
            found = INV_NEIGH * linear(s.ms_back[path], jnp.concatenate(hats, axis=1))
            for k in range(first, last):
                keep_wide(k + 1, found[:, (k - first) * atoms : (k - first + 1) * atoms])
            s.mixed_hat[(path + 1) * channels : (path + 2) * channels, :] = (
                slope * one + bend * mixed_dot * two
            )
        keep_wide(0, INV_NEIGH * linear(s.mf_back[...], s.mixed_hat[...]))

    def all_peers():
        return [far_peer(distance) for distance in range(group)] + [
            near_peer(distance) for distance in range(group - 1, 0, -1)
        ]

    def collect_messages(kind):
        total = s.msg_out[me]
        for other in all_peers():
            landed(s.msg_in.at[other], kind, other)
            total = total + s.msg_in[other]
        for other in all_peers():
            message_to(other, kind).wait_send()
        return INV_NEIGH * total

    def cotangent_to(other, kind):
        return remote(s.cot_all.at[me], s.cot_all.at[me], kind, other)

    def share_cotangent(value, kind):
        s.cot_all[me] = value
        for distance in range(1, group):
            cotangent_to(near_peer(distance), kind).start()
        for distance in range(group):
            cotangent_to(far_peer(distance), kind).start()

    def with_cotangents(number, kind, use):
        for distance in range(1, group):
            other = near_peer(distance)
            landed(s.cot_all.at[other], kind, other)
        use(number, half)
        for distance in range(group):
            other = far_peer(distance)
            landed(s.cot_all.at[other], kind, other)
        use(number, 1 - half)
        for other in all_peers():
            cotangent_to(other, kind).wait_send()

    def node_second_forward(number):
        agg = collect_messages(KIND_MSG)
        s.agg_two[number] = agg
        before = linear(s.ms_left[2], agg)
        s.last[number] = before
        gate = logistic(before)
        s.energy_row[...] = jnp.sum(
            s.readout_col[...] * (s.scalar[number] + before * gate), axis=0, keepdims=True
        )
        before_bar = s.readout_col[...] * silu_slope(before, gate)
        share_cotangent(INV_NEIGH * linear(s.ms_back[2], before_bar), KIND_COT)

    def node_second_second(number, energy_bar):
        all_early(number)
        agg_dot = collect_messages(KIND_TMSG)
        before = s.last[number]
        before_dot = linear(s.ms_left[2], agg_dot)
        gate = logistic(before)
        slope = silu_slope(before, gate)
        before_hat = s.readout_col[...] * (
            energy_bar * slope + silu_bend(before, gate) * before_dot
        )
        share_cotangent(INV_NEIGH * linear(s.ms_back[2], before_hat), KIND_TCOT)
        s.agg_two_dot[...] = agg_dot
        s.last_hat[...] = before_hat
        s.last_bar[...] = s.readout_col[...] * slope
        s.grad_ro[...] += energy_bar * (s.scalar[number] + before * gate) + (
            s.scalar_dot[...] + slope * before_dot
        )

    def share_rows(out_ref, in_ref, kind, meanwhile=None):
        def start(other):
            remote(out_ref, in_ref.at[me], kind, other).start()

        each_peer(start)
        in_ref[me] = out_ref[...]
        if meanwhile is not None:
            meanwhile()

        def wait(other):
            landed(in_ref.at[other], kind, other)
            remote(out_ref, in_ref.at[me], kind, other).wait_send()

        each_peer(wait)
        total = in_ref[0]
        for other in range(1, n_edge):
            total = total + in_ref[other]
        return total

    def evaluate(number):
        table(s.place)
        loop(2 * tiles, lambda index: geometry(number, index), True)
        s.sum_wide[...] = jnp.zeros_like(s.sum_wide)
        each_tile(lambda index: first_forward(number, index))
        node_first_forward(number)
        exchange_messages(number, KIND_MSG, second_forward)
        node_second_forward(number)
        s.sum_wide[...] = jnp.zeros_like(s.sum_wide)
        with_cotangents(number, KIND_COT, second_reverse)
        node_first_reverse(number)
        each_tile(lambda index: first_reverse(number, index))
        scatter_rows(number, s.force_out)
        s.force_out[3] = jnp.zeros((n_edge, atoms), F32)
        s.force_out[3, pl.ds(me, 1), :] = s.energy_row[...]

        def prepare():
            @pl.when(number < EVALS - 1)
            def _():
                one_hots(number + 1)

        total = share_rows(s.force_out, s.force_in, KIND_FORCE, prepare)
        force = -total[0:3]
        s.energy[number] = total[3]
        half_kick = 0.5 * STEP_DT * force

        @pl.when(number > 0)
        def _():
            s.speed[...] = s.speed[...] + half_kick

        @pl.when(number == 0)
        def _():
            s.start_kinetic[...] = 0.5 * jnp.sum(s.speed[...] * s.speed[...], axis=0)

        @pl.when(number < EVALS - 1)
        def _():
            s.speed[...] = s.speed[...] + half_kick
            s.place[...] = s.place[...] + STEP_DT * s.speed[...]

    one_hots(0)
    loop(EVALS, evaluate)

    kinetic = 0.5 * jnp.sum(s.speed[...] * s.speed[...], axis=0)
    change = (s.energy[EVALS - 1] + kinetic) - (s.energy[0] + s.start_kinetic[...])
    system_of = lax.broadcasted_iota(jnp.int32, (n_edge, atoms), 1) // half_atoms
    system_atoms = float(half_atoms * n_edge)
    loss = jnp.zeros((1, 1), F32)
    drift_grad = jnp.zeros((n_edge, atoms), F32)
    for number in range(SYS_LOC):
        mine = system_of == number
        drift = jnp.sum(jnp.where(mine, change, 0.0), axis=(0, 1), keepdims=True)
        loss = loss + drift * drift / system_atoms
        drift_grad = drift_grad + jnp.where(mine, 2.0 * drift / system_atoms, 0.0)
    s.drift_grad[...] = drift_grad
    s.place_bar[...] = jnp.zeros_like(s.place_bar)
    s.speed_bar[...] = drift_grad[None] * s.speed[...]
    s.loss_row[...] = jnp.broadcast_to(loss * jnp.where(me == 0, 1.0, 0.0), (1, channels))

    def reverse(step, last):
        number = EVALS - 1 - step
        sides = jnp.where(jnp.logical_or(number == 0, number == EVALS - 1), 1.0, 2.0)
        ends = jnp.where(number == 0, -1.0, jnp.where(number == EVALS - 1, 1.0, 0.0))
        s.move[...] = (-0.5 * STEP_DT * sides) * s.speed_bar[...]
        table(s.move)
        loop(2 * tiles, lambda index: geometry_tangent(number, index), True)
        energy_bar = ends * s.drift_grad[pl.ds(me, 1), :]
        s.sum_wide[...] = jnp.zeros_like(s.sum_wide)
        each_tile(lambda index: first_tangent(number, index))
        node_first_tangent(number)
        exchange_messages(number, KIND_TMSG, second_tangent)
        node_second_second(number, energy_bar)
        s.sum_wide[...] = jnp.zeros_like(s.sum_wide)
        with_cotangents(
            number, KIND_TCOT, lambda number, index: second_second(number, index, last)
        )
        node_first_second(number, energy_bar)
        if last:
            radial_gradients(1, number)
            node_gradients(number)
            pack_first()
            each_peer(lambda other: first_rows(other).start())
        each_tile(lambda index: first_second(number, index, last))
        if last:
            radial_gradients(0, number)
            kind_gradients(number)
            pack_second()
            each_peer(lambda other: second_rows(other).start())
        else:
            scatter_rows(number, s.place_out)

            def gradients():
                radial_gradients(1, number)
                node_gradients(number)
                radial_gradients(0, number)
                kind_gradients(number)

            total = share_rows(s.place_out, s.place_in, KIND_TFORCE, gradients)
            s.place_bar[...] = s.place_bar[...] + total
            s.speed_bar[...] = s.speed_bar[...] + STEP_DT * s.place_bar[...]

    first_each, second_each = [ref.shape[0] // n_edge for ref in (s.grad_first, s.grad_second)]

    def some_rows(ref, other, count):
        return ref.at[pl.ds(pl.multiple_of(other * count, 8), count)]

    def first_rows(other):
        return remote(
            some_rows(s.grad_first, other, first_each),
            s.part_in.at[me, 0:first_each],
            KIND_SCATTER,
            other,
        )

    def second_rows(other):
        return remote(
            some_rows(s.grad_second, other, second_each),
            s.part_in.at[me, first_each:],
            KIND_SCATTER_LATE,
            other,
        )

    def join_out(layer):
        found = s.grad_out[layer]
        rows = 3 * channels
        return found[0:rows, 0:channels] + found[0:rows, channels:] + found[rows:, 0:channels]

    def join_in(layer):
        found = s.grad_in[layer]
        return found[0:8, 0:channels] + found[0:8, channels:] + found[8:16, 0:channels]

    def pack_first():
        out = s.grad_first
        rows = 3 * channels
        out[0:rows, :] = jnp.concatenate([join_out(1), s.grad_mf[...]], axis=1)
        out[rows : rows + channels, :] = jnp.concatenate([s.grad_ms[0], s.grad_ms[1]], axis=1)
        ones = jnp.ones((8, atoms), BF)
        ro_rows = 0.0
        for piece in three_parts_f32(s.grad_ro[...]):
            ro_rows = ro_rows + dot_nt(ones, piece.astype(BF))
        rest = jnp.zeros((channels - 16, channels), F32)
        small = jnp.concatenate([ro_rows, join_in(1), rest], axis=0)
        out[rows + channels : rows + 2 * channels, :] = jnp.concatenate(
            [s.grad_ms[2], small], axis=1
        )

    def pack_second():
        out = s.grad_second
        rows = 3 * channels // 2
        found = join_out(0)
        out[0:rows, :] = jnp.concatenate([found[0:rows], found[rows:]], axis=1)
        out[rows : rows + 8, :] = jnp.concatenate([join_in(0), s.grad_emb[0:8, :]], axis=1)
        loss_rows = jnp.broadcast_to(s.loss_row[...], (8, channels))
        out[rows + 8 : rows + 16, :] = jnp.concatenate([loss_rows, loss_rows], axis=1)

    lax.fori_loop(0, EVALS - 1, lambda step, carry: (reverse(step, False), carry)[1], 0)
    reverse(EVALS - 1, True)

    s.part_in[me, 0:first_each, :] = some_rows(s.grad_first, me, first_each)[...]
    s.part_in[me, first_each:, :] = some_rows(s.grad_second, me, second_each)[...]

    def wait_scatter(other):
        landed(s.part_in.at[other, 0:first_each], KIND_SCATTER, other)
        landed(s.part_in.at[other, first_each:], KIND_SCATTER_LATE, other)
        first_rows(other).wait_send()
        second_rows(other).wait_send()

    each_peer(wait_scatter)
    total = s.part_in[0]
    for other in range(1, n_edge):
        total = total + s.part_in[other]
    s.sys_in[my_group] = total

    def line_copy(other, index):
        return pltpu.make_async_remote_copy(
            src_ref=s.sys_in.at[index],
            dst_ref=s.sys_in.at[index],
            send_sem=s.send_sem.at[KIND_SYS, other],
            recv_sem=s.recv_sem.at[KIND_SYS, index],
            device_id={"edge": 2 * other + core},
            device_id_type=MESH,
        )

    each_group(lambda other: line_copy(other, my_group).start())

    def wait_line(other):
        line_copy(other, other).wait_recv()
        line_copy(other, my_group).wait_send()

    each_group(wait_line)
    total = s.sys_in[0]
    for other in range(1, n_sys):
        total = total + s.sys_in[other]
    s.summed[me] = total
    mine = s.summed.at[me]
    each_peer(lambda other: remote(mine, mine, KIND_GATHER, other).start())

    def wait_gather(other):
        landed(s.summed.at[other], KIND_GATHER, other)
        remote(mine, mine, KIND_GATHER, other).wait_send()

    each_peer(wait_gather)
    first_total = s.grad_first.shape[0]
    for other in range(n_edge):
        total_ref[other * first_each : (other + 1) * first_each, :] = s.summed[other, 0:first_each, :]
        low_row = first_total + other * second_each
        total_ref[low_row : low_row + second_each, :] = s.summed[other, first_each:, :]


class Scratch:
    pass


def step_scratch(n_edge, n_sys, channels, atoms, first_rows, second_rows):
    tiles = TILES
    lanes = n_edge // tiles * atoms
    wide = N_COMP * channels
    vm = lambda *shape: pltpu.VMEM(shape, F32)
    vb = lambda *shape: pltpu.VMEM(shape, BF)
    vi = lambda *shape: pltpu.VMEM(shape, jnp.int32)
    return dict(
        send_sem=pltpu.SemaphoreType.DMA((KINDS, n_edge)),
        recv_sem=pltpu.SemaphoreType.DMA((KINDS, n_edge)),
        start_out=vm(8, atoms),
        start_float=vm(n_edge, 8, atoms),
        lists_own=vi(n_edge, 16, atoms),
        own_kind=vb(16, atoms),
        lists_out=vi(n_edge, 16, atoms),
        lists_in=vi(n_edge, 16, atoms),
        w_in_left=vb(2, channels, 32),
        w_in_back=vb(2, 16, 2 * channels),
        w_out_left=vb(2, 3 * channels, 3 * channels),
        w_out_back=vb(2, 2 * channels, 3 * channels),
        mf_left=vb(3 * channels, 3 * channels),
        mf_back=vb(channels, 9 * channels),
        ms_left=vb(3, channels, 3 * channels),
        ms_back=vb(3, channels, 3 * channels),
        emb_left=vb(channels, 48),
        readout_col=vm(channels, atoms),
        start_scalar=vm(channels, atoms),
        place=vm(3, n_edge, atoms),
        speed=vm(3, n_edge, atoms),
        energy_row=vm(1, atoms),
        energy=vm(EVALS, n_edge, atoms),
        start_kinetic=vm(n_edge, atoms),
        drift_grad=vm(n_edge, atoms),
        place_bar=vm(3, n_edge, atoms),
        speed_bar=vm(3, n_edge, atoms),
        move=vm(3, n_edge, atoms),
        own_hot=vb(EVALS, 2 * tiles, 2 * atoms, lanes),
        far_hot=vb(EVALS, 2 * tiles, atoms, lanes),
        kind_hot=vb(EVALS, tiles, 16, lanes),
        kind_value=vm(EVALS, tiles, channels, lanes),
        rows=vm(n_edge, 8, atoms),
        pieces=vb(n_edge, 32, atoms),
        row_own=vm(8, atoms),
        edge_rows=vm(2 * tiles, 8, lanes),
        geo=vm(EVALS, 2 * tiles, 40, lanes),
        geo_bar=vm(EVALS, 2 * tiles, 24, lanes),
        geo_dot=vm(2 * tiles, 24, lanes),
        hidden=vm(2, EVALS, tiles, channels, lanes),
        hidden_bar=vm(2, EVALS, tiles, channels, lanes),
        hidden_dot=vm(2, tiles, channels, lanes),
        radial=vm(2, EVALS, tiles, 3 * channels, lanes),
        radial_dot=vm(2, tiles, 3 * channels, lanes),
        m_high=vb(tiles, wide, lanes),
        m_low=vb(tiles, wide, lanes),
        r_pair=vb(2, tiles, 6 * channels, lanes),
        h_pair=vb(2, tiles, 6 * channels, lanes),
        out_pair=vb(2, tiles, 2 * channels, lanes),
        hat_pair=vb(2, tiles, 2 * channels, lanes),
        scalar_hat=vm(channels, atoms),
        raw_hat=vm(8 * channels, atoms),
        last_hat=vm(channels, atoms),
        last_bar=vm(channels, atoms),
        agg_two_dot=vm(channels, atoms),
        loss_row=vm(1, channels),
        v_high=vb(tiles, channels, lanes),
        v_low=vb(tiles, channels, lanes),
        a_pair=vb(wide, 2 * atoms),
        sum_wide=vm(wide, atoms),
        first_cot=vm(EVALS, tiles, wide, lanes),
        feat=vm(EVALS, tiles, wide, lanes),
        feat_dot=vm(tiles, wide, lanes),
        along=vm(EVALS, tiles, 2 * channels, lanes),
        along_dot=vm(tiles, 2 * channels, lanes),
        msg_cot=vm(EVALS, tiles, channels, lanes),
        msg_hat=vm(tiles, channels, lanes),
        agg=vm(EVALS, wide, atoms),
        agg_dot=vm(wide, atoms),
        mixed=vm(EVALS, 3 * channels, atoms),
        mixed_dot=vm(3 * channels, atoms),
        mixed_bar=vm(EVALS, 3 * channels, atoms),
        mixed_hat=vm(3 * channels, atoms),
        raw=vm(EVALS, 8 * channels, atoms),
        raw_dot=vm(8 * channels, atoms),
        raw_bar=vm(EVALS, 8 * channels, atoms),
        scalar=vm(EVALS, channels, atoms),
        scalar_dot=vm(channels, atoms),
        feat_bar=vm(EVALS, wide, atoms),
        agg_two=vm(EVALS, channels, atoms),
        last=vm(EVALS, channels, atoms),
        msg_out=vm(n_edge, channels, atoms),
        msg_in=vm(n_edge, channels, atoms),
        cot_all=vm(n_edge, channels, atoms),
        force_out=vm(4, n_edge, atoms),
        force_in=vm(n_edge, 4, n_edge, atoms),
        place_out=vm(3, n_edge, atoms),
        place_in=vm(n_edge, 3, n_edge, atoms),
        grad_emb=vm(16, channels),
        grad_in=vm(2, 2 * NB, 2 * channels),
        grad_out=vm(2, 6 * channels, 2 * channels),
        grad_mf=vm(3 * channels, channels),
        grad_ms=vm(3, channels, channels),
        grad_ro=vm(channels, atoms),
        grad_first=vm(first_rows, 2 * channels),
        grad_second=vm(second_rows, 2 * channels),
        part_in=vm(n_edge, (first_rows + second_rows) // n_edge, 2 * channels),
        sys_in=vm(n_sys, (first_rows + second_rows) // n_edge, 2 * channels),
        summed=vm(n_edge, (first_rows + second_rows) // n_edge, 2 * channels),
    )


def gradient_rows(n_edge, channels):
    unit = 8 * n_edge
    return -(-(5 * channels) // unit) * unit, -(-(3 * channels // 2 + 16) // unit) * unit


def whole_step(positions, velocities, species, senders, receivers, edge_mask, params):
    n_edge, n_sys = lax.axis_size("edge"), lax.axis_size("sys")
    atoms = positions.shape[1]
    channels = params[0].shape[1]
    first_rows, second_rows = gradient_rows(n_edge, channels)
    shapes = step_scratch(n_edge, n_sys, channels, atoms, first_rows, second_rows)
    names = tuple(shapes)

    def kernel(*refs):
        scratch = Scratch()
        for name, ref in zip(names, refs[13:]):
            setattr(scratch, name, ref)
        step_kernel(n_edge, n_sys, *refs[:13], scratch)

    embedding, radial_in, radial_out, mix_first, mix_square, readout = params
    operands = (
        positions,
        velocities,
        species,
        senders,
        receivers,
        edge_mask,
        embedding,
        radial_in,
        radial_out,
        mix_first,
        mix_square,
        readout,
    )
    return pl.pallas_call(
        kernel,
        out_shape=jax.ShapeDtypeStruct((first_rows + second_rows, 2 * channels), F32),
        in_specs=[pl.BlockSpec(memory_space=pltpu.VMEM)] * len(operands),
        out_specs=pl.BlockSpec(memory_space=pltpu.VMEM),
        scratch_shapes=list(shapes.values()),
        compiler_params=pltpu.CompilerParams(
            collective_id=0, has_side_effects=True, vmem_limit_bytes=60 * 1024 * 1024
        ),
    )(*operands)


def to_column(row):
    count = row.shape[1]
    square = jnp.broadcast_to(row, (count, count))
    same = lax.broadcasted_iota(jnp.int32, (count, count), 0) == lax.broadcasted_iota(
        jnp.int32, (count, count), 1
    )
    return jnp.sum(jnp.where(same, square, 0.0), axis=1, keepdims=True)


def to_row(column):
    count = column.shape[0]
    square = jnp.broadcast_to(column, (count, count))
    same = lax.broadcasted_iota(jnp.int32, (count, count), 0) == lax.broadcasted_iota(
        jnp.int32, (count, count), 1
    )
    return jnp.sum(jnp.where(same, square, 0.0), axis=0, keepdims=True)


def total_mean(value):
    return jnp.sum(
        jnp.sum(value, axis=1, keepdims=True), axis=0, keepdims=True
    ) / float(value.shape[0] * value.shape[1])


def factored_rows(gradient, weight, row_state, col_state):
    decay_rate = 1.0 - STEP_NUM ** (-0.8)
    squares = gradient * gradient + EPS_SQUARE
    size_m, size_n = gradient.shape
    row_mean = jnp.sum(squares, axis=1, keepdims=True) / float(size_n)
    col_mean = jnp.sum(squares, axis=0, keepdims=True) / float(size_m)
    row_new = decay_rate * to_column(row_state) + (1.0 - decay_rate) * row_mean
    col_new = decay_rate * col_state + (1.0 - decay_rate) * col_mean
    second = row_new * col_new / total_mean(row_new)
    weight_rms = jnp.sqrt(total_mean(weight * weight) + 1e-06)
    weight_new = weight - RELATIVE * weight_rms * gradient * lax.rsqrt(second)
    return (gradient, to_row(row_new), col_new, weight_new, weight_new.astype(jnp.bfloat16))


def update_kernel(total_ref, *refs):
    weights, states, outs = refs[0:6], refs[6:17], refs[17:]
    kinds, channels = weights[0].shape

    rows = 3 * channels
    late = gradient_rows(lax.axis_size("edge"), channels)[0]
    small = rows + channels
    first_layer = jnp.concatenate(
        [
            total_ref[late : late + rows // 2, :channels],
            total_ref[late : late + rows // 2, channels:],
        ],
        axis=0,
    )
    below = late + rows // 2
    gradients = (
        [total_ref[below : below + kinds, channels:]],
        [total_ref[below : below + 8, :channels], total_ref[small + 8 : small + 16, channels:]],
        [first_layer.T, total_ref[0:rows, :channels].T],
        [total_ref[0:rows, channels:].T],
        [
            total_ref[rows:small, :channels],
            total_ref[rows:small, channels:],
            total_ref[small : small + channels, :channels],
        ],
    )
    outs[0][...] = total_ref[below + 8 : below + 9, 0:1]
    for which, parts in enumerate(gradients):
        weight, rows, cols = weights[which], states[2 * which], states[2 * which + 1]
        results = outs[1 + 5 * which : 6 + 5 * which]
        stacked = len(weight.shape) == 3
        for number, gradient in enumerate(parts):
            if stacked:
                found = factored_rows(
                    gradient,
                    weight[number],
                    rows[number : number + 1, :],
                    cols[number : number + 1, :],
                )
                results[0][number] = found[0]
                results[1][number : number + 1, :] = found[1]
                results[2][number : number + 1, :] = found[2]
                results[3][number] = found[3]
                results[4][number] = found[4]
            else:
                size_m, size_n = weight.shape
                found = factored_rows(
                    gradient,
                    weight[...],
                    rows[...].reshape(1, size_m),
                    cols[...].reshape(1, size_n),
                )
                results[0][...] = found[0]
                results[1][...] = found[1].reshape(size_m)
                results[2][...] = found[2].reshape(size_n)
                results[3][...] = found[3]
                results[4][...] = found[4]
    gradient = total_ref[small : small + 1, channels:]
    decay_rate = 1.0 - STEP_NUM ** (-0.8)
    weight = weights[5][...].reshape(1, channels)
    second_new = decay_rate * states[10][...].reshape(1, channels) + (1.0 - decay_rate) * (
        gradient * gradient + EPS_SQUARE
    )
    weight_rms = jnp.sqrt(total_mean(weight * weight) + 1e-06)
    weight_new = weight - RELATIVE * weight_rms * gradient * lax.rsqrt(second_new)
    outs[26][...] = gradient.reshape(channels)
    outs[27][...] = second_new.reshape(channels)
    outs[28][...] = weight_new.reshape(channels)
    outs[29][...] = weight_new.astype(jnp.bfloat16).reshape(channels)


def whole_update(total, params, states):
    shapes = [jax.ShapeDtypeStruct((1, 1), F32)]
    for which in range(5):
        weight, rows, cols = params[which], states[2 * which], states[2 * which + 1]
        for like in (weight, rows, cols, weight):
            shapes.append(jax.ShapeDtypeStruct(like.shape, F32))
        shapes.append(jax.ShapeDtypeStruct(weight.shape, jnp.bfloat16))
    for kind in (F32, F32, F32, jnp.bfloat16):
        shapes.append(jax.ShapeDtypeStruct(params[5].shape, kind))
    operands = (total, *params, *states)
    results = pl.pallas_call(
        update_kernel,
        out_shape=shapes,
        in_specs=[pl.BlockSpec(memory_space=pltpu.VMEM)] * len(operands),
        out_specs=[pl.BlockSpec(memory_space=pltpu.VMEM)] * len(shapes),
        compiler_params=pltpu.CompilerParams(vmem_limit_bytes=8 * 1024 * 1024),
    )(*operands)
    return (results[0].reshape(()), *results[1:])


def fits_kernel(senders, atom_count):
    n_edge = lax.axis_size("edge")
    slots = senders.shape[1] // n_edge
    whole = slots == atom_count and atom_count % 128 == 0
    even = n_edge & (n_edge - 1) == 0 and n_edge >= 2 * TILES
    return whole and even and n_edge == 2 * lax.axis_size("sys")


def on_device(
    positions,
    velocities,
    species,
    senders,
    receivers,
    edge_mask,
    embedding,
    radial_in,
    radial_out,
    mix_first,
    mix_square,
    readout,
    embedding_rows,
    embedding_cols,
    radial_in_rows,
    radial_in_cols,
    radial_out_rows,
    radial_out_cols,
    mix_first_rows,
    mix_first_cols,
    mix_square_rows,
    mix_square_cols,
    readout_second,
):
    params = (embedding, radial_in, radial_out, mix_first, mix_square, readout)
    atom_count = positions.shape[1]
    states = (
        embedding_rows,
        embedding_cols,
        radial_in_rows,
        radial_in_cols,
        radial_out_rows,
        radial_out_cols,
        mix_first_rows,
        mix_first_cols,
        mix_square_rows,
        mix_square_cols,
        readout_second,
    )
    if fits_kernel(senders, atom_count):
        total = whole_step(
            positions, velocities, species, senders, receivers, edge_mask, params
        )
        return whole_update(total, params, states)
    spec_hot = (species[None, :] == jnp.arange(embedding.shape[0])[:, None]).astype(jnp.float32)
    edge_lists = receivers[None]
    arrived = lax.all_to_all(edge_lists, "edge", split_axis=2, concat_axis=2, tiled=True)
    passes = [
        build(senders[number], arrived[:, number], edge_mask[number], atom_count, spec_hot)
        for number in range(EVALS)
    ]
    coords = positions
    moving = velocities
    energies, forces, stored = passes[0][0](coords, params)
    record = [stored]
    first_energy = energies
    for number in range(STEPS):
        half_speed = moving + 0.5 * STEP_DT * forces
        coords = coords + STEP_DT * half_speed
        energies, forces, stored = passes[number + 1][0](coords, params)
        record.append(stored)
        moving = half_speed + 0.5 * STEP_DT * forces
    local_sums = jnp.stack(
        [
            per_system(first_energy),
            per_system(energies),
            per_system(0.5 * jnp.sum(velocities * velocities, axis=0)),
            per_system(0.5 * jnp.sum(moving * moving, axis=0)),
        ]
    )
    totals = lax.psum(local_sums, "edge")
    drift = totals[1] + totals[3] - (totals[0] + totals[2])
    system_atoms = atom_count // SYS_LOC * lax.axis_size("edge")
    loss_local = jnp.sum(drift * drift) / system_atoms
    drift_grad = jnp.repeat(2.0 * drift / system_atoms, atom_count // SYS_LOC)
    speed_bar = drift_grad[None, :] * moving
    coord_bar = jnp.zeros_like(positions)
    force_next = jnp.zeros_like(positions)
    gradients = jax.tree.map(jnp.zeros_like, params)
    for number in reversed(range(STEPS)):
        later = number + 1
        force_bar = force_next + 0.5 * STEP_DT * speed_bar
        if later == STEPS:
            energy_bar = drift_grad
        else:
            energy_bar = jnp.zeros_like(drift_grad)
        coord_part, param_part = passes[later][1](record[later], params, energy_bar, force_bar)
        gradients = add_trees([gradients, param_part])
        coord_bar = coord_bar + coord_part
        half_bar = speed_bar + STEP_DT * coord_bar
        speed_bar = half_bar
        force_next = 0.5 * STEP_DT * half_bar
    _, param_part = passes[0][1](record[0], params, -drift_grad, force_next)
    gradients = add_trees([gradients, param_part])
    loss_term = loss_local * (lax.axis_index("edge") == 0).astype(jnp.float32)
    summed = lax.psum(
        (
            gradients[0],
            gradients[1],
            gradients[2],
            gradients[3],
            gradients[4],
            gradients[5],
            loss_term,
        ),
        ("sys", "edge"),
    )
    return update(summed, params, states)


def solution(mesh):
    placed = (
        P(None, ("sys", "edge")),
        P(None, ("sys", "edge")),
        P(("sys", "edge")),
        P(None, ("sys", "edge")),
        P(None, ("sys", "edge")),
        P(None, ("sys", "edge")),
        P(),
        P(),
        P(),
        P(),
        P(),
        P(),
        P(),
        P(),
        P(),
        P(),
        P(),
        P(),
        P(),
        P(),
        P(),
        P(),
        P(),
    )
    return jax.shard_map(
        on_device,
        mesh=mesh,
        in_specs=placed,
        out_specs=(
            P(),
            P(),
            P(),
            P(),
            P(),
            P(),
            P(),
            P(),
            P(),
            P(),
            P(),
            P(),
            P(),
            P(),
            P(),
            P(),
            P(),
            P(),
            P(),
            P(),
            P(),
            P(),
            P(),
            P(),
            P(),
            P(),
            P(),
            P(),
            P(),
            P(),
        ),
        check_vma=False,
    )
```

profile of v0, /device:TPU:0, one launch (start us, length us, event | category | flops | bytes accessed | tf_op | source)
XLA Modules:
  0.0 157.7 jit_solution(9884033218576423532)
XLA Ops:
  0.7 0.0 copy-start.9
  0.7 0.0 copy-start.2
  0.7 0.0 copy-start.3
  0.7 0.0 copy-start.1
  0.7 0.0 copy-start.4
  0.7 0.0 copy-start.5
  0.7 0.0 copy-start.17
  0.8 0.0 copy-start.8
  0.8 0.0 copy-start.7
  0.8 0.0 copy-start.13
  0.8 0.0 copy-start.16
  0.8 0.0 copy-start.6
  0.8 0.0 copy-start.12
  0.8 0.0 copy-start.11
  0.8 0.0 copy-start.10
  0.8 0.0 copy-start.15
  0.8 0.0 copy-start.14
  0.8 153.7 %shard_map.454.total_ref = f32[448,128]{1,0:T(8,128)} custom-call(f32[3,128]{1,0:T(4,128)} %refs_0_.2, f32[3,128]{1,0:T(4,128)} %refs_1_.2, s32[128]{0:T(128)} %refs_2_.2, s32[3,1024]{1,0:T(4,128)} %refs_3_.2, s32[3,1024]{1,0:T(4,128)} %refs_4_.2, s32[3,1024]{1,0:T(4,128)} %refs_5_.2, f32[4,64]{1,0:T(4,128)} %refs_0_.3, f32[2,8,64]{2,1,0:T(8,128)} %refs_1_.3, ...), custom_call_target="tpu_custom_call" | custom-call | tf_op jit(solution)/shard_map/pallas_call | solution.py:1919
  154.6 0.0 copy-done.9
  154.6 0.0 copy-done.2
  154.6 0.0 copy-done.3
  154.6 0.0 copy-done.1
  154.6 0.0 copy-done.4
  154.6 0.0 copy-done.5
  154.6 0.0 copy-done.17
  154.6 0.0 copy-done.8
  154.7 0.0 copy-done.7
  154.7 0.0 copy-done.13
  154.7 0.0 copy-done.16
  154.7 0.0 copy-done.6
  154.7 0.0 copy-done.12
  154.7 0.0 copy-done.11
  154.7 0.0 copy-done.10
  154.7 0.0 copy-done.15
  154.7 0.0 copy-done.14
  154.7 0.0 copy-start
  154.8 0.9 copy-done
  155.7 1.8 %shard_map.455 = (f32[1,1]{1,0:T(1,128)}, f32[4,64]{1,0:T(4,128)}, f32[4]{0:T(128)}, f32[64]{0:T(128)}, f32[4,64]{1,0:T(4,128)}, /*index=5*/bf16[4,64]{1,0:T(4,1...) custom-call(f32[448,128]{1,0:T(8,128)S(1)} %copy-done, ...), custom_call_target="tpu_custom_call" | custom-call | tf_op jit(solution)/shard_map/pallas_call | solution.py:2050
Async XLA Ops:
  0.7 153.9 %copy-start.9 = (f32[64]{0:T(128)S(1)}, f32[64]{0:T(128)}, u32[]{:S(2)}) copy-start(f32[64]{0:T(128)} %refs_5_.3) | copy-start | bytes 772
  0.7 153.9 %copy-start.2 = (f32[3,64,64]{2,1,0:T(8,128)S(1)}, f32[3,64,64]{2,1,0:T(8,128)}, u32[]{:S(2)}) copy-start(f32[3,64,64]{2,1,0:T(8,128)} %refs_4_.3) | copy-start | bytes 147460
  0.7 153.9 %copy-start.3 = (f32[64,192]{1,0:T(8,128)S(1)}, f32[64,192]{1,0:T(8,128)}, u32[]{:S(2)}) copy-start(f32[64,192]{1,0:T(8,128)} %refs_3_.3) | copy-start | bytes 147460
  0.7 153.9 %copy-start.1 = (f32[2,64,192]{2,1,0:T(8,128)S(1)}, f32[2,64,192]{2,1,0:T(8,128)}, u32[]{:S(2)}) copy-start(f32[2,64,192]{2,1,0:T(8,128)} %refs_2_.3) | copy-start | bytes 294916
  0.7 153.9 %copy-start.4 = (f32[2,8,64]{2,1,0:T(8,128)S(1)}, f32[2,8,64]{2,1,0:T(8,128)}, u32[]{:S(2)}) copy-start(f32[2,8,64]{2,1,0:T(8,128)} %refs_1_.3) | copy-start | bytes 12292
  0.7 153.9 %copy-start.5 = (f32[4,64]{1,0:T(4,128)S(1)}, f32[4,64]{1,0:T(4,128)}, u32[]{:S(2)}) copy-start(f32[4,64]{1,0:T(4,128)} %refs_0_.3) | copy-start | bytes 3076
  0.7 153.9 %copy-start.17 = (f32[64]{0:T(128)S(1)}, f32[64]{0:T(128)}, u32[]{:S(2)}) copy-start(f32[64]{0:T(128)} %refs_16_.1) | copy-start | bytes 772
  0.8 153.9 %copy-start.8 = (f32[3,64]{1,0:T(4,128)S(1)}, f32[3,64]{1,0:T(4,128)}, u32[]{:S(2)}) copy-start(f32[3,64]{1,0:T(4,128)} %refs_15_.1) | copy-start | bytes 2308
  0.8 153.9 %copy-start.7 = (f32[3,64]{1,0:T(4,128)S(1)}, f32[3,64]{1,0:T(4,128)}, u32[]{:S(2)}) copy-start(f32[3,64]{1,0:T(4,128)} %refs_14_.1) | copy-start | bytes 2308
  0.8 153.9 %copy-start.13 = (f32[192]{0:T(256)S(1)}, f32[192]{0:T(256)}, u32[]{:S(2)}) copy-start(f32[192]{0:T(256)} %refs_13_.1) | copy-start | bytes 2308
  0.8 153.9 %copy-start.16 = (f32[64]{0:T(128)S(1)}, f32[64]{0:T(128)}, u32[]{:S(2)}) copy-start(f32[64]{0:T(128)} %refs_12_.1) | copy-start | bytes 772
  0.8 153.9 %copy-start.6 = (f32[2,192]{1,0:T(2,128)S(1)}, f32[2,192]{1,0:T(2,128)}, u32[]{:S(2)}) copy-start(f32[2,192]{1,0:T(2,128)} %refs_11_.3) | copy-start | bytes 4612
  0.8 153.9 %copy-start.12 = (f32[2,64]{1,0:T(2,128)S(1)}, f32[2,64]{1,0:T(2,128)}, u32[]{:S(2)}) copy-start(f32[2,64]{1,0:T(2,128)} %refs_10_.3) | copy-start | bytes 1540
  0.8 153.9 %copy-start.11 = (f32[2,64]{1,0:T(2,128)S(1)}, f32[2,64]{1,0:T(2,128)}, u32[]{:S(2)}) copy-start(f32[2,64]{1,0:T(2,128)} %refs_9_.3) | copy-start | bytes 1540
  0.8 153.9 %copy-start.10 = (f32[2,8]{1,0:T(2,128)S(1)}, f32[2,8]{1,0:T(2,128)}, u32[]{:S(2)}) copy-start(f32[2,8]{1,0:T(2,128)} %refs_8_.3) | copy-start | bytes 196
  0.8 153.9 %copy-start.15 = (f32[64]{0:T(128)S(1)}, f32[64]{0:T(128)}, u32[]{:S(2)}) copy-start(f32[64]{0:T(128)} %refs_7_.3) | copy-start | bytes 772
  0.8 153.9 %copy-start.14 = (f32[4]{0:T(128)S(1)}, f32[4]{0:T(128)}, u32[]{:S(2)}) copy-start(f32[4]{0:T(128)} %refs_6_.3) | copy-start | bytes 52
  154.7 0.9 copy-start
where the time goes:
time: 158 us
  Pallas kernels  156 us (99%)
    pallas_call x1, Pallas kernels, whole_step(): pl.pallas_call(kernel, out_shape=jax.ShapeDtypeStruct((first_rows + secon...  154 us

commit v1 on v0

--- a/solution.py
+++ b/solution.py
@@ -1012,7 +1012,6 @@
 
     def all_early(number):
         for index in range(tiles):
-            second_early(number, index)
             first_early(number, index)
         for first, last, path in PATHS:
             bars = [s.raw_bar[number, k * channels : (k + 1) * channels, :] for k in range(first, last)]
@@ -1051,7 +1050,8 @@
         ref[chunk_at((3 + path) * channels, c), lane] = low
 
     def add_scatter(index, hot):
-        s.sum_wide[...] += dot_nt(s.m_high[index], hot) + dot_nt(s.m_low[index], hot)
+        found = dot_nt(jnp.concatenate([s.m_high[index], s.m_low[index]], axis=0), hot)
+        s.sum_wide[...] += found[0:wide] + found[wide:]
 
     def harmonic_rows(ref, lane):
         return [ref[row : row + 1, lane] for row in range(8)]
@@ -1214,9 +1214,9 @@
         for part in range(group):
             at = slice(part * atoms, (part + 1) * atoms)
             hot = s.far_hot[number, index, :, at]
-            s.msg_out[index * group + part] = dot_nt(s.v_high[index, :, at], hot) + dot_nt(
-                s.v_low[index, :, at], hot
-            )
+            pair = jnp.concatenate([s.v_high[index, :, at], s.v_low[index, :, at]], axis=0)
+            found = dot_nt(pair, hot)
+            s.msg_out[index * group + part] = found[0:channels] + found[channels:]
 
     def near_peer(distance):
         return half * group + jnp.bitwise_xor(lax.rem(me, group), distance)
@@ -1524,7 +1524,8 @@
         share_cotangent(INV_NEIGH * linear(s.ms_back[2], before_bar), KIND_COT)
 
     def node_second_second(number, energy_bar):
-        all_early(number)
+        for index in range(tiles):
+            second_early(number, index)
         agg_dot = collect_messages(KIND_TMSG)
         before = s.last[number]
         before_dot = linear(s.ms_left[2], agg_dot)
@@ -1631,6 +1632,7 @@
         node_first_tangent(number)
         exchange_messages(number, KIND_TMSG, second_tangent)
         node_second_second(number, energy_bar)
+        all_early(number)
         s.sum_wide[...] = jnp.zeros_like(s.sum_wide)
         with_cotangents(
             number, KIND_TCOT, lambda number, index: second_second(number, index, last)

time: 158 us -> 157 us (level)
  no operation moved by 1% of the time
where the time goes in v1:
time: 157 us
  Pallas kernels  155 us (99%)
    pallas_call x1, Pallas kernels, whole_step(): pl.pallas_call(kernel, out_shape=jax.ShapeDtypeStruct((first_rows + secon...  153 us

profile of v1, /device:TPU:0, one launch (start us, length us, event | category | flops | bytes accessed | tf_op | source)
XLA Modules:
  0.0 157.0 jit_solution(6897750346846526868)
XLA Ops:
  0.7 0.0 copy-start.9
  0.7 0.0 copy-start.2
  0.7 0.0 copy-start.3
  0.7 0.0 copy-start.1
  0.7 0.0 copy-start.4
  0.7 0.0 copy-start.5
  0.7 0.0 copy-start.17
  0.8 0.0 copy-start.8
  0.8 0.0 copy-start.7
  0.8 0.0 copy-start.13
  0.8 0.0 copy-start.16
  0.8 0.0 copy-start.6
  0.8 0.0 copy-start.12
  0.8 0.0 copy-start.11
  0.8 0.0 copy-start.10
  0.8 0.0 copy-start.15
  0.8 0.0 copy-start.14
  0.8 153.0 %shard_map.454.total_ref = f32[448,128]{1,0:T(8,128)} custom-call(f32[3,128]{1,0:T(4,128)} %refs_0_.2, f32[3,128]{1,0:T(4,128)} %refs_1_.2, s32[128]{0:T(128)} %refs_2_.2, s32[3,1024]{1,0:T(4,128)} %refs_3_.2, s32[3,1024]{1,0:T(4,128)} %refs_4_.2, s32[3,1024]{1,0:T(4,128)} %refs_5_.2, f32[4,64]{1,0:T(4,128)} %refs_0_.3, f32[2,8,64]{2,1,0:T(8,128)} %refs_1_.3, ...), custom_call_target="tpu_custom_call" | custom-call | tf_op jit(solution)/shard_map/pallas_call | solution.py:1921
  153.9 0.0 copy-done.9
  153.9 0.0 copy-done.2
  153.9 0.0 copy-done.3
  153.9 0.0 copy-done.1
  153.9 0.0 copy-done.4
  153.9 0.0 copy-done.5
  153.9 0.0 copy-done.17
  153.9 0.0 copy-done.8
  153.9 0.0 copy-done.7
  153.9 0.0 copy-done.13
  154.0 0.0 copy-done.16
  154.0 0.0 copy-done.6
  154.0 0.0 copy-done.12
  154.0 0.0 copy-done.11
  154.0 0.0 copy-done.10
  154.0 0.0 copy-done.15
  154.0 0.0 copy-done.14
  154.0 0.0 copy-start
  154.0 0.9 copy-done
  155.0 1.8 %shard_map.455 = (f32[1,1]{1,0:T(1,128)}, f32[4,64]{1,0:T(4,128)}, f32[4]{0:T(128)}, f32[64]{0:T(128)}, f32[4,64]{1,0:T(4,128)}, /*index=5*/bf16[4,64]{1,0:T(4,1...) custom-call(f32[448,128]{1,0:T(8,128)S(1)} %copy-done, ...), custom_call_target="tpu_custom_call" | custom-call | tf_op jit(solution)/shard_map/pallas_call | solution.py:2052
Async XLA Ops:
  0.7 153.2 %copy-start.9 = (f32[64]{0:T(128)S(1)}, f32[64]{0:T(128)}, u32[]{:S(2)}) copy-start(f32[64]{0:T(128)} %refs_5_.3) | copy-start | bytes 772
  0.7 153.2 %copy-start.2 = (f32[3,64,64]{2,1,0:T(8,128)S(1)}, f32[3,64,64]{2,1,0:T(8,128)}, u32[]{:S(2)}) copy-start(f32[3,64,64]{2,1,0:T(8,128)} %refs_4_.3) | copy-start | bytes 147460
  0.7 153.2 %copy-start.3 = (f32[64,192]{1,0:T(8,128)S(1)}, f32[64,192]{1,0:T(8,128)}, u32[]{:S(2)}) copy-start(f32[64,192]{1,0:T(8,128)} %refs_3_.3) | copy-start | bytes 147460
  0.7 153.2 %copy-start.1 = (f32[2,64,192]{2,1,0:T(8,128)S(1)}, f32[2,64,192]{2,1,0:T(8,128)}, u32[]{:S(2)}) copy-start(f32[2,64,192]{2,1,0:T(8,128)} %refs_2_.3) | copy-start | bytes 294916
  0.7 153.2 %copy-start.4 = (f32[2,8,64]{2,1,0:T(8,128)S(1)}, f32[2,8,64]{2,1,0:T(8,128)}, u32[]{:S(2)}) copy-start(f32[2,8,64]{2,1,0:T(8,128)} %refs_1_.3) | copy-start | bytes 12292
  0.7 153.2 %copy-start.5 = (f32[4,64]{1,0:T(4,128)S(1)}, f32[4,64]{1,0:T(4,128)}, u32[]{:S(2)}) copy-start(f32[4,64]{1,0:T(4,128)} %refs_0_.3) | copy-start | bytes 3076
  0.7 153.2 %copy-start.17 = (f32[64]{0:T(128)S(1)}, f32[64]{0:T(128)}, u32[]{:S(2)}) copy-start(f32[64]{0:T(128)} %refs_16_.1) | copy-start | bytes 772
  0.8 153.2 %copy-start.8 = (f32[3,64]{1,0:T(4,128)S(1)}, f32[3,64]{1,0:T(4,128)}, u32[]{:S(2)}) copy-start(f32[3,64]{1,0:T(4,128)} %refs_15_.1) | copy-start | bytes 2308
  0.8 153.2 %copy-start.7 = (f32[3,64]{1,0:T(4,128)S(1)}, f32[3,64]{1,0:T(4,128)}, u32[]{:S(2)}) copy-start(f32[3,64]{1,0:T(4,128)} %refs_14_.1) | copy-start | bytes 2308
  0.8 153.2 %copy-start.13 = (f32[192]{0:T(256)S(1)}, f32[192]{0:T(256)}, u32[]{:S(2)}) copy-start(f32[192]{0:T(256)} %refs_13_.1) | copy-start | bytes 2308
  0.8 153.2 %copy-start.16 = (f32[64]{0:T(128)S(1)}, f32[64]{0:T(128)}, u32[]{:S(2)}) copy-start(f32[64]{0:T(128)} %refs_12_.1) | copy-start | bytes 772
  0.8 153.2 %copy-start.6 = (f32[2,192]{1,0:T(2,128)S(1)}, f32[2,192]{1,0:T(2,128)}, u32[]{:S(2)}) copy-start(f32[2,192]{1,0:T(2,128)} %refs_11_.3) | copy-start | bytes 4612
  0.8 153.2 %copy-start.12 = (f32[2,64]{1,0:T(2,128)S(1)}, f32[2,64]{1,0:T(2,128)}, u32[]{:S(2)}) copy-start(f32[2,64]{1,0:T(2,128)} %refs_10_.3) | copy-start | bytes 1540
  0.8 153.2 %copy-start.11 = (f32[2,64]{1,0:T(2,128)S(1)}, f32[2,64]{1,0:T(2,128)}, u32[]{:S(2)}) copy-start(f32[2,64]{1,0:T(2,128)} %refs_9_.3) | copy-start | bytes 1540
  0.8 153.2 %copy-start.10 = (f32[2,8]{1,0:T(2,128)S(1)}, f32[2,8]{1,0:T(2,128)}, u32[]{:S(2)}) copy-start(f32[2,8]{1,0:T(2,128)} %refs_8_.3) | copy-start | bytes 196
  0.8 153.2 %copy-start.15 = (f32[64]{0:T(128)S(1)}, f32[64]{0:T(128)}, u32[]{:S(2)}) copy-start(f32[64]{0:T(128)} %refs_7_.3) | copy-start | bytes 772
  0.8 153.2 %copy-start.14 = (f32[4]{0:T(128)S(1)}, f32[4]{0:T(128)}, u32[]{:S(2)}) copy-start(f32[4]{0:T(128)} %refs_6_.3) | copy-start | bytes 52
  154.0 0.9 copy-start
